TPU v7x, 256 devices: a whole 4x4x8 slice. The times are simulated.
256 devices in a mesh: gx: 32 (over y, z_hi, core), gy: 8 (over z_lo, x).
Axes of the slice: x: 4, y: 4, z: 8 (z_hi: 4, z_lo: 2; z = z_hi * 2 + z_lo), core: 2. Of those that a mesh axis runs over, the one named last changes fastest.
Arguments:
- level_set: float32 [256, 64, 256], P('gx', 'gy'), may hold values from -6 to 6
- source: float32 [256, 64, 256], P('gx', 'gy'), may hold values from -8 to 8
- stiffness: float32 [256, 64, 256], P('gx', 'gy'), may hold values from 0.1 to 6
- snap_buffer: bfloat16 [8, 64, 16, 64], P(None, 'gx', 'gy'), may hold values from -4 to 4
- buffer_order: int32 [8], replicated, may hold values from 0 to 7, each once
- first_weight: bfloat16 [27, 64], replicated, may hold values from -1.25 to 1.25
- second_weight: bfloat16 [1728, 64], replicated, may hold values from -0.15625 to 0.15625
- out_grad: bfloat16 [8, 64, 16, 4096], P('gy', 'gx'), may hold values from -0.15625 to 0.15625
Outputs:
- new_level: float32 [256, 64, 256], P('gx', 'gy')
- pressure: float32 [256, 64, 256], P('gx', 'gy')
- dw_first: float32 [27, 64], replicated
- dw_second: float32 [1728, 64], replicated
Inputs may be any that keep to these rules, and one draw needn't show every extreme that they name: buffer_order holds every slot of 0 to 7 once.
All inputs are finite; a program needn't handle non-finite values.
Results may differ from a plain program's by a relative error of at most 0.0035.
Values may be sent and summed in bfloat16 or wider, within the bound.
A program may use at most 64 MiB of HBM per device.

v0:
```python
import jax
import jax.numpy as jnp
from jax import lax
from jax.sharding import PartitionSpec as P

COARSEN = 4
ITERS = 20


time_step = 2.0


def padded_2(block, sides, width):
    for axis, dim in sides:
        count = lax.axis_size(axis)
        forward = [(i, i + 1) for i in range(count - 1)]
        backward = [(target, source) for source, target in forward]
        low = lax.ppermute(
            lax.slice_in_dim(block, block.shape[dim] - width, None, axis=dim), axis, forward
        )
        high = lax.ppermute(lax.slice_in_dim(block, 0, width, axis=dim), axis, backward)
        block = jnp.concatenate([low, block, high], axis=dim)
    return block


def neighbours(padded):
    total = padded[2:, 1:-1, 1:-1] + padded[:-2, 1:-1, 1:-1]
    total = total + padded[1:-1, 2:, 1:-1] + padded[1:-1, :-2, 1:-1]
    return total + padded[1:-1, 1:-1, 2:] + padded[1:-1, 1:-1, :-2]


def advance(p_pad, f_pad, level):
    grad_px = 0.5 * (p_pad[2:, 1:-1, 1:-1] - p_pad[:-2, 1:-1, 1:-1])
    grad_py = 0.5 * (p_pad[1:-1, 2:, 1:-1] - p_pad[1:-1, :-2, 1:-1])
    grad_pz = 0.5 * (p_pad[1:-1, 1:-1, 2:] - p_pad[1:-1, 1:-1, :-2])
    grad_fx = 0.5 * (f_pad[2:, 1:-1, 1:-1] - f_pad[:-2, 1:-1, 1:-1])
    grad_fy = 0.5 * (f_pad[1:-1, 2:, 1:-1] - f_pad[1:-1, :-2, 1:-1])
    grad_fz = 0.5 * (f_pad[1:-1, 1:-1, 2:] - f_pad[1:-1, 1:-1, :-2])
    return level + time_step * (grad_px * grad_fx + grad_py * grad_fy + grad_pz * grad_fz)


def tile_faces(field):
    extended = padded_2(field, (("gx", 0), ("gy", 1)), 1)
    return jnp.pad(extended, ((0, 0), (0, 0), (1, 1)))


def level_stack(padded, nx, ny, nz):
    rows = []
    for dx in range(3):
        for dy in range(3):
            for dz in range(3):
                rows.append(padded[:, dx : dx + nx, dy : dy + ny, dz : dz + nz].reshape(-1))
    return jnp.stack(rows, 0)


def first_layer(stack, weight):
    return lax.dot_general(
        stack, weight, (((0,), (0,)), ((), ())), preferred_element_type=jnp.float32
    )


def second_grad(h_pad, g_flat, nx, ny, nz):
    blocks = []
    for dx in range(3):
        for dy in range(3):
            block = jnp.concatenate(
                [h_pad[:, dx : dx + nx, dy : dy + ny, dz : dz + nz, :] for dz in range(3)], axis=-1
            )
            block = block.reshape(-1, block.shape[-1])
            blocks.append(
                lax.dot_general(
                    block, g_flat, (((0,), (0,)), ((), ())), preferred_element_type=jnp.float32
                )
            )
    return jnp.concatenate(blocks, 0)


def back_features(g_pad, weight, nx, ny, nz):
    chans = g_pad.shape[-1]
    total = jnp.zeros((g_pad.shape[0] * nx * ny * nz, chans), jnp.float32)
    for dx in range(3):
        for dy in range(3):
            block = jnp.concatenate(
                [
                    g_pad[:, 2 - dx : 2 - dx + nx, 2 - dy : 2 - dy + ny, 2 - dz : 2 - dz + nz, :]
                    for dz in range(3)
                ],
                axis=-1,
            )
            block = block.reshape(-1, 3 * chans)
            mats = []
            for dz in range(3):
                off = dx * 9 + dy * 3 + dz
                mats.append(weight[off * chans : (off + 1) * chans, :].T)
            total = total + jnp.dot(
                block, jnp.concatenate(mats, 0), preferred_element_type=jnp.float32
            )
    return total


def silu_slope(z):
    sig = jax.nn.sigmoid(z)
    return sig * (1.0 + z * (1.0 - sig))


def pad_sides(field):
    widths = [(0, 0), (0, 0), (1, 1), (1, 1)] + [(0, 0)] * (field.ndim - 4)
    return jnp.pad(field, widths)


def per_device(
    level_set, source, stiffness, snap_buffer, buffer_order, first_weight, second_weight, out_grad
):

    def sweep(i, press):
        return (source + neighbours(tile_faces(press))) / (6.0 + stiffness)

    pressure = lax.fori_loop(0, ITERS, sweep, jnp.zeros_like(source))
    new_level = advance(tile_faces(pressure), tile_faces(level_set), level_set)
    tile_x, tile_y, tile_z = level_set.shape
    coarse = new_level.reshape(
        tile_x // COARSEN, COARSEN, tile_y // COARSEN, COARSEN, tile_z // COARSEN, COARSEN
    )
    coarse = coarse.mean(axis=(1, 3, 5)).astype(jnp.bfloat16)
    chosen = (jnp.arange(snap_buffer.shape[0], dtype=jnp.int32) == buffer_order[0])[
        :, None, None, None
    ]
    updated = jnp.where(chosen, coarse[None], snap_buffer)
    local_snaps = jnp.take(updated, buffer_order, axis=0)
    snaps = lax.all_to_all(local_snaps, "gy", split_axis=0, concat_axis=2, tiled=True)
    held, nx, ny, nz = snaps.shape
    chans = first_weight.shape[1]
    level_ext = padded_2(snaps, (("gx", 1),), 1)
    stack = level_stack(pad_sides(level_ext), nx, ny, nz)
    z_one = first_layer(stack, first_weight)
    h_one = jax.nn.silu(z_one).astype(jnp.bfloat16).reshape(held, nx, ny, nz * chans)
    h_ext = padded_2(h_one, (("gx", 1),), 1)
    h_pad = pad_sides(h_ext.reshape(held, nx + 2, ny, nz, chans))
    grad_ext = padded_2(out_grad, (("gx", 1),), 1)
    g_pad = pad_sides(grad_ext.reshape(held, nx + 2, ny, nz, chans))
    g_flat = out_grad.reshape(-1, chans)
    dw_two = second_grad(h_pad, g_flat, nx, ny, nz)
    dh_one = back_features(g_pad, second_weight, nx, ny, nz)
    dz_one = (dh_one * silu_slope(z_one)).astype(jnp.bfloat16)
    dw_one = jnp.dot(stack, dz_one, preferred_element_type=jnp.float32)
    dw_first, dw_second = lax.psum((dw_one, dw_two), ("gx", "gy"))
    return (new_level, pressure, dw_first, dw_second)


def solution(mesh):
    placed = (
        P("gx", "gy", None),
        P("gx", "gy", None),
        P("gx", "gy", None),
        P(None, "gx", "gy", None),
        P(),
        P(),
        P(),
        P("gy", "gx", None, None),
    )
    return jax.shard_map(
        per_device,
        mesh=mesh,
        in_specs=placed,
        out_specs=(P("gx", "gy", None), P("gx", "gy", None), P(), P()),
        check_vma=False,
    )
```

profile of v0, /device:TPU:1, one launch (start us, length us, event | category | flops | bytes accessed | tf_op | source)
XLA Modules:
  0.0 799.5 jit_solution(17139841607486464167)
XLA Ops:
  7.9 6.3 collective-permute-start.7
  16.2 381.5 %while.13 = (s32[]{:T(128)}, f32[8,8,256]{2,1,0:T(8,128)S(1)}, f32[8,8,256]{2,1,0:T(8,128)}, f32[8,8,256]{2,1,0:T(8,128)}, s32[]{:T(128)}, /*index=5*/s32[]{:T(128)}) while((s32[]{:T(128)}, f32[8,8,256]{2,1,0:T(8,128)S(1)}, f32[8,8,256]{2,1,0:T(8,128)}, f32[8,8,256]{2,1,0:T(8,128)}, s32[]{:T(128)}, /*index=5*/s32[]{:T(128)}) %tuple.151), condition=%wide.region_1.2_spmd.clone, body=%wide.region_0.1_spmd.clone.sunk | while | flops 598371 | bytes 1049615 | solution.py:118
  18.3 4.5 collective-permute-start.1
  32.8 6.2 collective-permute-start.1
  41.2 4.5 collective-permute-start.3
  49.7 5.9 collective-permute-start.1
  66.2 5.9 collective-permute-start.1
  82.7 6.7 collective-permute-start.1
  91.5 6.4 collective-permute-start.3
  101.8 7.2 collective-permute-start.1
  111.1 6.7 collective-permute-start.3
  121.7 7.2 collective-permute-start.1
  131.0 6.7 collective-permute-start.3
  141.6 7.2 collective-permute-start.1
  150.8 6.7 collective-permute-start.3
  161.4 7.2 collective-permute-start.1
  170.7 6.7 collective-permute-start.3
  181.3 7.2 collective-permute-start.1
  190.5 6.7 collective-permute-start.3
  201.1 7.2 collective-permute-start.1
  210.4 6.7 collective-permute-start.3
  221.0 7.2 collective-permute-start.1
  230.2 6.7 collective-permute-start.3
  240.8 7.2 collective-permute-start.1
  250.1 6.7 collective-permute-start.3
  260.7 7.2 collective-permute-start.1
  269.9 6.7 collective-permute-start.3
  280.5 7.2 collective-permute-start.1
  289.8 6.7 collective-permute-start.3
  300.4 7.2 collective-permute-start.1
  309.6 6.7 collective-permute-start.3
  320.2 7.2 collective-permute-start.1
  329.5 6.7 collective-permute-start.3
  340.1 7.2 collective-permute-start.1
  349.4 6.7 collective-permute-start.3
  360.0 7.2 collective-permute-start.1
  369.2 6.7 collective-permute-start.3
  379.8 7.2 collective-permute-start.1
  389.1 6.7 collective-permute-start.3
  397.7 7.2 collective-permute-start.5
  408.9 6.3 collective-permute-start.14
  416.6 6.7 collective-permute-start.11
  424.6 6.7 collective-permute-start.9
  436.3 13.4 %all-to-all-start = ((bf16[8,2,128]{2,1,0:T(2,128)(2,1)}), bf16[8,2,128]{2,1,0:T(2,128)(2,1)S(1)}, u32[]{:S(2)}, u32[]{:S(2)}) async-start(bf16[8,2,128]{2,1,0:T(2,128)(2,1)} %reshape.125), calls=%async_computation | async-start | bytes 8192 | tf_op jit(solution)/shard_map/all_to_all | solution.py:130
  456.7 10.5 %collective-permute-start.12 = (bf16[1,1,16,64]{3,2,1,0:T(8,128)(2,1)S(1)}, bf16[1,1,16,64]{3,2,1,0:T(8,128)(2,1)S(1)}, u32[]{:S(2)}, u32[]{:S(2)}) collective-permute-start(bf16[1,1,16,64]{3,2,1,0:T(8,128)(2,1)S(1)} %get-tuple-element.203), channel_id=1, source_target_pairs={{0,8},{8,16},{16,24},{24,32},{32,40},{40,48},{48,56},{56,64},{64,7... | collective-permute-start | bytes 6152 | tf_op jit(solution)/shard_map/ppermute | solution.py:18
  476.7 4.5 collective-permute-start.16
  522.1 98.5 %psum.14 = f32[27,64]{1,0:T(8,128)} all-reduce(f32[27,64]{1,0:T(8,128)S(1)} %fusion.14), channel_id=1, replica_groups=mesh['gx'=32,'gy'=8] {'gx','gy'}, use_global_device_ids=true, to_apply=%region_3.4 | all-reduce | flops 1728 | bytes 13824 | tf_op jit(solution)/shard_map/psum | solution.py:146
  620.6 170.2 %all-reduce.8.cloned.1.call-done = f32[1728,64]{0,1:T(8,128)} async-done(((f32[1728,64]{0,1:T(8,128)}), f32[1728,64]{0,1:T(8,128)}) %all-reduce.8.cloned.1.call-update) | async-done | bytes 442384 | tf_op jit(solution)/shard_map/psum | solution.py:146
  (455 shorter events, 204.9 us)
Async XLA Ops:
  7.9 401.0 %collective-permute-start.7 = (f32[1,8,256]{2,1,0:T(8,128)S(1)}, f32[1,8,256]{2,1,0:T(8,128)S(1)}, u32[]{:S(2)}, u32[]{:S(2)}) collective-permute-start(f32[1,8,256]{2,1,0:T(8,128)S(1)} %get-tuple-element.176), channel_id=1, source_target_pairs={{0,8},{8,16},{16,24},{24,32},{32,40},{40,48},{48,56},{56,64},{64,7... | collective-permute-start | bytes 24584 | tf_op jit(solution)/shard_map/ppermute | solution.py:18
  14.2 401.0 %collective-permute-start.6 = (f32[1,8,256]{2,1,0:T(8,128)S(1)}, f32[1,8,256]{2,1,0:T(8,128)S(1)}, u32[]{:S(2)}, u32[]{:S(2)}) collective-permute-start(f32[1,8,256]{2,1,0:T(8,128)S(1)} %get-tuple-element.175), channel_id=1, source_target_pairs={{8,0},{16,8},{24,16},{32,24},{40,32},{48,40},{56,48},{64,56},{72,6... | collective-permute-start | bytes 24584 | tf_op jit(solution)/shard_map/ppermute | solution.py:21
  30.9 8.2 %collective-permute-start = (f32[1,8,256]{2,1,0:T(8,128)S(1)}, f32[1,8,256]{2,1,0:T(8,128)S(1)}, u32[]{:S(2)}, u32[]{:S(2)}) collective-permute-start(f32[1,8,256]{2,1,0:T(8,128)S(1)} %get-tuple-element.249), channel_id=1, source_target_pairs={{8,0},{16,8},{24,16},{32,24},{40,32},{48,40},{56,48},{64,56},{72,6... | collective-permute-start | bytes 24584 | tf_op jit(solution)/shard_map/while/body/eval_jaxpr/ppermute | solution.py:21
  80.8 8.7 %collective-permute-start = (f32[1,8,256]{2,1,0:T(8,128)S(1)}, f32[1,8,256]{2,1,0:T(8,128)S(1)}, u32[]{:S(2)}, u32[]{:S(2)}) collective-permute-start(f32[1,8,256]{2,1,0:T(8,128)S(1)} %get-tuple-element.249), channel_id=1, source_target_pairs={{8,0},{16,8},{24,16},{32,24},{40,32},{48,40},{56,48},{64,56},{72,6... | collective-permute-start | bytes 24584 | tf_op jit(solution)/shard_map/while/body/eval_jaxpr/ppermute | solution.py:21
  99.9 9.1 %collective-permute-start = (f32[1,8,256]{2,1,0:T(8,128)S(1)}, f32[1,8,256]{2,1,0:T(8,128)S(1)}, u32[]{:S(2)}, u32[]{:S(2)}) collective-permute-start(f32[1,8,256]{2,1,0:T(8,128)S(1)} %get-tuple-element.249), channel_id=1, source_target_pairs={{8,0},{16,8},{24,16},{32,24},{40,32},{48,40},{56,48},{64,56},{72,6... | collective-permute-start | bytes 24584 | tf_op jit(solution)/shard_map/while/body/eval_jaxpr/ppermute | solution.py:21
  109.8 8.0 collective-permute-start.2
  119.8 9.1 %collective-permute-start = (f32[1,8,256]{2,1,0:T(8,128)S(1)}, f32[1,8,256]{2,1,0:T(8,128)S(1)}, u32[]{:S(2)}, u32[]{:S(2)}) collective-permute-start(f32[1,8,256]{2,1,0:T(8,128)S(1)} %get-tuple-element.249), channel_id=1, source_target_pairs={{8,0},{16,8},{24,16},{32,24},{40,32},{48,40},{56,48},{64,56},{72,6... | collective-permute-start | bytes 24584 | tf_op jit(solution)/shard_map/while/body/eval_jaxpr/ppermute | solution.py:21
  129.7 8.0 collective-permute-start.2
  139.6 9.1 %collective-permute-start = (f32[1,8,256]{2,1,0:T(8,128)S(1)}, f32[1,8,256]{2,1,0:T(8,128)S(1)}, u32[]{:S(2)}, u32[]{:S(2)}) collective-permute-start(f32[1,8,256]{2,1,0:T(8,128)S(1)} %get-tuple-element.249), channel_id=1, source_target_pairs={{8,0},{16,8},{24,16},{32,24},{40,32},{48,40},{56,48},{64,56},{72,6... | collective-permute-start | bytes 24584 | tf_op jit(solution)/shard_map/while/body/eval_jaxpr/ppermute | solution.py:21
  141.6 7.9 collective-permute-start.1
  149.5 8.0 collective-permute-start.2
  159.5 9.1 %collective-permute-start = (f32[1,8,256]{2,1,0:T(8,128)S(1)}, f32[1,8,256]{2,1,0:T(8,128)S(1)}, u32[]{:S(2)}, u32[]{:S(2)}) collective-permute-start(f32[1,8,256]{2,1,0:T(8,128)S(1)} %get-tuple-element.249), channel_id=1, source_target_pairs={{8,0},{16,8},{24,16},{32,24},{40,32},{48,40},{56,48},{64,56},{72,6... | collective-permute-start | bytes 24584 | tf_op jit(solution)/shard_map/while/body/eval_jaxpr/ppermute | solution.py:21
  169.4 8.0 collective-permute-start.2
  179.3 9.1 %collective-permute-start = (f32[1,8,256]{2,1,0:T(8,128)S(1)}, f32[1,8,256]{2,1,0:T(8,128)S(1)}, u32[]{:S(2)}, u32[]{:S(2)}) collective-permute-start(f32[1,8,256]{2,1,0:T(8,128)S(1)} %get-tuple-element.249), channel_id=1, source_target_pairs={{8,0},{16,8},{24,16},{32,24},{40,32},{48,40},{56,48},{64,56},{72,6... | collective-permute-start | bytes 24584 | tf_op jit(solution)/shard_map/while/body/eval_jaxpr/ppermute | solution.py:21
  189.2 8.0 collective-permute-start.2
  199.2 9.1 %collective-permute-start = (f32[1,8,256]{2,1,0:T(8,128)S(1)}, f32[1,8,256]{2,1,0:T(8,128)S(1)}, u32[]{:S(2)}, u32[]{:S(2)}) collective-permute-start(f32[1,8,256]{2,1,0:T(8,128)S(1)} %get-tuple-element.249), channel_id=1, source_target_pairs={{8,0},{16,8},{24,16},{32,24},{40,32},{48,40},{56,48},{64,56},{72,6... | collective-permute-start | bytes 24584 | tf_op jit(solution)/shard_map/while/body/eval_jaxpr/ppermute | solution.py:21
  209.1 8.0 collective-permute-start.2
  219.0 9.1 %collective-permute-start = (f32[1,8,256]{2,1,0:T(8,128)S(1)}, f32[1,8,256]{2,1,0:T(8,128)S(1)}, u32[]{:S(2)}, u32[]{:S(2)}) collective-permute-start(f32[1,8,256]{2,1,0:T(8,128)S(1)} %get-tuple-element.249), channel_id=1, source_target_pairs={{8,0},{16,8},{24,16},{32,24},{40,32},{48,40},{56,48},{64,56},{72,6... | collective-permute-start | bytes 24584 | tf_op jit(solution)/shard_map/while/body/eval_jaxpr/ppermute | solution.py:21
  228.9 8.0 collective-permute-start.2
  238.9 9.1 %collective-permute-start = (f32[1,8,256]{2,1,0:T(8,128)S(1)}, f32[1,8,256]{2,1,0:T(8,128)S(1)}, u32[]{:S(2)}, u32[]{:S(2)}) collective-permute-start(f32[1,8,256]{2,1,0:T(8,128)S(1)} %get-tuple-element.249), channel_id=1, source_target_pairs={{8,0},{16,8},{24,16},{32,24},{40,32},{48,40},{56,48},{64,56},{72,6... | collective-permute-start | bytes 24584 | tf_op jit(solution)/shard_map/while/body/eval_jaxpr/ppermute | solution.py:21
  248.8 8.0 collective-permute-start.2
  258.8 9.1 %collective-permute-start = (f32[1,8,256]{2,1,0:T(8,128)S(1)}, f32[1,8,256]{2,1,0:T(8,128)S(1)}, u32[]{:S(2)}, u32[]{:S(2)}) collective-permute-start(f32[1,8,256]{2,1,0:T(8,128)S(1)} %get-tuple-element.249), channel_id=1, source_target_pairs={{8,0},{16,8},{24,16},{32,24},{40,32},{48,40},{56,48},{64,56},{72,6... | collective-permute-start | bytes 24584 | tf_op jit(solution)/shard_map/while/body/eval_jaxpr/ppermute | solution.py:21
  268.6 8.0 collective-permute-start.2
  278.6 9.1 %collective-permute-start = (f32[1,8,256]{2,1,0:T(8,128)S(1)}, f32[1,8,256]{2,1,0:T(8,128)S(1)}, u32[]{:S(2)}, u32[]{:S(2)}) collective-permute-start(f32[1,8,256]{2,1,0:T(8,128)S(1)} %get-tuple-element.249), channel_id=1, source_target_pairs={{8,0},{16,8},{24,16},{32,24},{40,32},{48,40},{56,48},{64,56},{72,6... | collective-permute-start | bytes 24584 | tf_op jit(solution)/shard_map/while/body/eval_jaxpr/ppermute | solution.py:21
  288.5 8.0 collective-permute-start.2
  298.5 9.1 %collective-permute-start = (f32[1,8,256]{2,1,0:T(8,128)S(1)}, f32[1,8,256]{2,1,0:T(8,128)S(1)}, u32[]{:S(2)}, u32[]{:S(2)}) collective-permute-start(f32[1,8,256]{2,1,0:T(8,128)S(1)} %get-tuple-element.249), channel_id=1, source_target_pairs={{8,0},{16,8},{24,16},{32,24},{40,32},{48,40},{56,48},{64,56},{72,6... | collective-permute-start | bytes 24584 | tf_op jit(solution)/shard_map/while/body/eval_jaxpr/ppermute | solution.py:21
  308.3 8.0 collective-permute-start.2
  318.3 9.1 %collective-permute-start = (f32[1,8,256]{2,1,0:T(8,128)S(1)}, f32[1,8,256]{2,1,0:T(8,128)S(1)}, u32[]{:S(2)}, u32[]{:S(2)}) collective-permute-start(f32[1,8,256]{2,1,0:T(8,128)S(1)} %get-tuple-element.249), channel_id=1, source_target_pairs={{8,0},{16,8},{24,16},{32,24},{40,32},{48,40},{56,48},{64,56},{72,6... | collective-permute-start | bytes 24584 | tf_op jit(solution)/shard_map/while/body/eval_jaxpr/ppermute | solution.py:21
  328.2 8.0 collective-permute-start.2
  338.2 9.1 %collective-permute-start = (f32[1,8,256]{2,1,0:T(8,128)S(1)}, f32[1,8,256]{2,1,0:T(8,128)S(1)}, u32[]{:S(2)}, u32[]{:S(2)}) collective-permute-start(f32[1,8,256]{2,1,0:T(8,128)S(1)} %get-tuple-element.249), channel_id=1, source_target_pairs={{8,0},{16,8},{24,16},{32,24},{40,32},{48,40},{56,48},{64,56},{72,6... | collective-permute-start | bytes 24584 | tf_op jit(solution)/shard_map/while/body/eval_jaxpr/ppermute | solution.py:21
  348.1 8.0 collective-permute-start.2
  358.0 9.1 %collective-permute-start = (f32[1,8,256]{2,1,0:T(8,128)S(1)}, f32[1,8,256]{2,1,0:T(8,128)S(1)}, u32[]{:S(2)}, u32[]{:S(2)}) collective-permute-start(f32[1,8,256]{2,1,0:T(8,128)S(1)} %get-tuple-element.249), channel_id=1, source_target_pairs={{8,0},{16,8},{24,16},{32,24},{40,32},{48,40},{56,48},{64,56},{72,6... | collective-permute-start | bytes 24584 | tf_op jit(solution)/shard_map/while/body/eval_jaxpr/ppermute | solution.py:21
  367.9 8.0 collective-permute-start.2
  377.9 9.1 %collective-permute-start = (f32[1,8,256]{2,1,0:T(8,128)S(1)}, f32[1,8,256]{2,1,0:T(8,128)S(1)}, u32[]{:S(2)}, u32[]{:S(2)}) collective-permute-start(f32[1,8,256]{2,1,0:T(8,128)S(1)} %get-tuple-element.249), channel_id=1, source_target_pairs={{8,0},{16,8},{24,16},{32,24},{40,32},{48,40},{56,48},{64,56},{72,6... | collective-permute-start | bytes 24584 | tf_op jit(solution)/shard_map/while/body/eval_jaxpr/ppermute | solution.py:21
  387.8 8.0 collective-permute-start.2
  397.7 18.8 %collective-permute-start.5 = (f32[1,8,256]{2,1,0:T(8,128)S(1)}, f32[1,8,256]{2,1,0:T(8,128)S(1)}, u32[]{:S(2)}, u32[]{:S(2)}) collective-permute-start(f32[1,8,256]{2,1,0:T(8,128)S(1)} %get-tuple-element.174), channel_id=1, source_target_pairs={{0,8},{8,16},{16,24},{24,32},{32,40},{40,48},{48,56},{56,64},{64,7... | collective-permute-start | bytes 24584 | tf_op jit(solution)/shard_map/ppermute | solution.py:18
  404.9 18.4 %collective-permute-start.4 = (f32[1,8,256]{2,1,0:T(8,128)S(1)}, f32[1,8,256]{2,1,0:T(8,128)S(1)}, u32[]{:S(2)}, u32[]{:S(2)}) collective-permute-start(f32[1,8,256]{2,1,0:T(8,128)S(1)} %get-tuple-element.173), channel_id=1, source_target_pairs={{8,0},{16,8},{24,16},{32,24},{40,32},{48,40},{56,48},{64,56},{72,6... | collective-permute-start | bytes 24584 | tf_op jit(solution)/shard_map/ppermute | solution.py:21
  406.9 74.4 %collective-permute-start.15 = (bf16[1,1,16,4096]{3,2,1,0:T(8,128)(2,1)S(1)}, bf16[1,1,16,4096]{3,2,1,0:T(8,128)(2,1)}, u32[]{:S(2)}, u32[]{:S(2)}) collective-permute-start(bf16[1,1,16,4096]{3,2,1,0:T(8,128)(2,1)S(1)} %get-tuple-element.141), channel_id=1, source_target_pairs={{8,0},{16,8},{24,16},{32,24},{40,32},{48,40},{56,48},{64,56},{72,6... | collective-permute-start | bytes 393224 | tf_op jit(solution)/shard_map/ppermute | solution.py:21
  408.9 72.3 %collective-permute-start.14 = (bf16[1,1,16,4096]{3,2,1,0:T(8,128)(2,1)S(1)}, bf16[1,1,16,4096]{3,2,1,0:T(8,128)(2,1)}, u32[]{:S(2)}, u32[]{:S(2)}) collective-permute-start(bf16[1,1,16,4096]{3,2,1,0:T(8,128)(2,1)S(1)} %get-tuple-element.140), channel_id=1, source_target_pairs={{0,8},{8,16},{16,24},{24,32},{32,40},{40,48},{48,56},{56,64},{64,7... | collective-permute-start | bytes 393224 | tf_op jit(solution)/shard_map/ppermute | solution.py:18
  415.2 9.3 %collective-permute-start.10 = (f32[10,1,256]{2,1,0:T(1,128)S(1)}, f32[10,1,256]{2,1,0:T(1,128)S(1)}, u32[]{:S(2)}, u32[]{:S(2)}) collective-permute-start(f32[10,1,256]{2,1,0:T(1,128)S(1)} %get-tuple-element.172), channel_id=1, source_target_pairs={{1,0},{2,1},{3,2},{4,3},{5,4},{6,5},{7,6},{9,8},{10,9},{11,10},{12... | collective-permute-start | bytes 30728 | tf_op jit(solution)/shard_map/ppermute | solution.py:21
  416.6 14.7 %collective-permute-start.11 = (f32[10,1,256]{2,1,0:T(1,128)S(1)}, f32[10,1,256]{2,1,0:T(1,128)S(1)}, u32[]{:S(2)}, u32[]{:S(2)}) collective-permute-start(f32[10,1,256]{2,1,0:T(1,128)S(1)} %get-tuple-element.171), channel_id=1, source_target_pairs={{0,1},{1,2},{2,3},{3,4},{4,5},{5,6},{6,7},{8,9},{9,10},{10,11},{11... | collective-permute-start | bytes 30728 | tf_op jit(solution)/shard_map/ppermute | solution.py:18
  423.3 8.2 %collective-permute-start.8 = (f32[10,1,256]{2,1,0:T(1,128)S(1)}, f32[10,1,256]{2,1,0:T(1,128)S(1)}, u32[]{:S(2)}, u32[]{:S(2)}) collective-permute-start(f32[10,1,256]{2,1,0:T(1,128)S(1)} %get-tuple-element.170), channel_id=1, source_target_pairs={{1,0},{2,1},{3,2},{4,3},{5,4},{6,5},{7,6},{9,8},{10,9},{11,10},{12... | collective-permute-start | bytes 30728 | tf_op jit(solution)/shard_map/ppermute | solution.py:21
  436.3 18.3 %all-to-all-start = ((bf16[8,2,128]{2,1,0:T(2,128)(2,1)}), bf16[8,2,128]{2,1,0:T(2,128)(2,1)S(1)}, u32[]{:S(2)}, u32[]{:S(2)}) async-start(bf16[8,2,128]{2,1,0:T(2,128)(2,1)} %reshape.125), calls=%async_computation | async-start | bytes 8192 | tf_op jit(solution)/shard_map/all_to_all | solution.py:130
  449.7 341.2 %all-reduce.8.cloned.1.call-start = ((), (), s32[]{:S(2)}) async-start(), calls=%async_computation.1 | async-start | bytes 917504 | tf_op jit(solution)/shard_map/psum | solution.py:146
  454.8 13.8 %collective-permute-start.13 = (bf16[1,1,16,64]{3,2,1,0:T(8,128)(2,1)S(1)}, bf16[1,1,16,64]{3,2,1,0:T(8,128)(2,1)S(1)}, u32[]{:S(2)}, u32[]{:S(2)}) collective-permute-start(bf16[1,1,16,64]{3,2,1,0:T(8,128)(2,1)S(1)} %get-tuple-element.204), channel_id=1, source_target_pairs={{8,0},{16,8},{24,16},{32,24},{40,32},{48,40},{56,48},{64,56},{72,6... | collective-permute-start | bytes 6152 | tf_op jit(solution)/shard_map/ppermute | solution.py:21
  456.7 11.9 %collective-permute-start.12 = (bf16[1,1,16,64]{3,2,1,0:T(8,128)(2,1)S(1)}, bf16[1,1,16,64]{3,2,1,0:T(8,128)(2,1)S(1)}, u32[]{:S(2)}, u32[]{:S(2)}) collective-permute-start(bf16[1,1,16,64]{3,2,1,0:T(8,128)(2,1)S(1)} %get-tuple-element.203), channel_id=1, source_target_pairs={{0,8},{8,16},{16,24},{24,32},{32,40},{40,48},{48,56},{56,64},{64,7... | collective-permute-start | bytes 6152 | tf_op jit(solution)/shard_map/ppermute | solution.py:18
  474.7 25.1 %collective-permute-start.17 = (bf16[1,1,16,4096]{3,2,1,0:T(8,128)(2,1)}, bf16[1,1,16,4096]{3,2,1,0:T(8,128)(2,1)S(1)}, u32[]{:S(2)}, u32[]{:S(2)}) collective-permute-start(bf16[1,1,16,4096]{3,2,1,0:T(8,128)(2,1)} %get-tuple-element.139), channel_id=1, source_target_pairs={{8,0},{16,8},{24,16},{32,24},{40,32},{48,40},{56,48},{64,56},{72,6... | collective-permute-start | bytes 393224 | tf_op jit(solution)/shard_map/ppermute | solution.py:21
  476.7 23.4 %collective-permute-start.16 = (bf16[1,1,16,4096]{3,2,1,0:T(8,128)(2,1)S(1)}, bf16[1,1,16,4096]{3,2,1,0:T(8,128)(2,1)S(1)}, u32[]{:S(2)}, u32[]{:S(2)}) collective-permute-start(bf16[1,1,16,4096]{3,2,1,0:T(8,128)(2,1)S(1)} %get-tuple-element.138), channel_id=1, source_target_pairs={{0,8},{8,16},{16,24},{24,32},{32,40},{40,48},{48,56},{56,64},{64,7... | collective-permute-start | bytes 393224 | tf_op jit(solution)/shard_map/ppermute | solution.py:18
  (98 other events, 2111.1 us)
Sparse Core Ops, SparseCore 0:
  521.2 269.6 all-reduce.7
where the time goes:
time: 804 us; the launch traced here: 800 us
  starting transfers between devices  398 us (50%)
  waiting for transfers between devices  206 us (26%)
  blocking collectives  98.5 us (12%)
  other arithmetic  38 us (5%)
  local copies, waits for them, and re-layouts  31.3 us (4%)
  between operations  15.1 us (2%)
  matrix products  10.3 us (1%)
    ppermute x47, starting transfers between devices, padded_2(): lax.ppermute(lax.slice_in_dim(block, block.shape[dim] - width, None, axis...  308 us
    psum x1, waiting for transfers between devices, per_device(): dw_first, dw_second = lax.psum((dw_one, dw_two), ('gx', 'gy'))  170 us
    psum x1, blocking collectives, per_device(): dw_first, dw_second = lax.psum((dw_one, dw_two), ('gx', 'gy'))  98.5 us
    ppermute x47, starting transfers between devices, padded_2(): lax.ppermute(lax.slice_in_dim(block, 0, width, axis=dim), axis, backward)  76.6 us
    ppermute x47, waiting for transfers between devices, padded_2(): lax.ppermute(lax.slice_in_dim(block, block.shape[dim] - width, None, axis...  31.5 us
    div x20, other arithmetic, sweep(): return (source + neighbours(tile_faces(press))) / (6.0 + stiffness)  19.4 us
  transfers between devices with their start and end apart: 96, of which 43 were waited for; matrix products, arithmetic and copies ran while one was open for 7% of the time, Pallas kernels for 0%

commit v1 on v0

v1 whole, which is shorter than its diff:
```python
import functools

import jax
import jax.numpy as jnp
from jax import lax
from jax.experimental import pallas as pl
from jax.experimental.pallas import tpu as pltpu
from jax.sharding import PartitionSpec as P

F32 = jnp.float32
BF16 = jnp.bfloat16
MESH = pl.DeviceIdType.MESH
GX, GY = 32, 8
FZ = 256
T = 8
ROWS = 512
RAD = 6
GROUP = 32
CHUNKS = 28
ZS = 8
DIRS = [(dx, dy) for dx in (-1, 0, 1) for dy in (-1, 0, 1) if (dx, dy) != (0, 0)]


def dot(a, b, dims=((1,), (0,)), precision=None):
    return lax.dot_general(
        a, b, (dims, ((), ())), preferred_element_type=F32, precision=precision
    )


def iota(shape, dim):
    return lax.broadcasted_iota(jnp.int32, shape, dim)


def row_before(v):
    y = iota(v.shape, 0) & 15
    return jnp.where(y == 0, 0.0, pltpu.roll(v, 1, 0))


def row_after(v):
    y = iota(v.shape, 0) & 15
    return jnp.where(y == 15, 0.0, pltpu.roll(v, v.shape[0] - 1, 0))


def z_before(v, axis):
    z = iota(v.shape, axis)
    return jnp.where(z == 0, 0.0, pltpu.roll(v, 1, axis))


def z_after(v, axis):
    z = iota(v.shape, axis)
    return jnp.where(z == FZ - 1, 0.0, pltpu.roll(v, FZ - 1, axis))


def kernel(
    src, stf, lev, snp, order, w1, w2, g,
    newl, prs, dw1o, dw2o,
    A, B, PP, absend, abrcv, psend, prcv, fysend, fxr, fyr,
    snsend, snrcv, grcv, W, GT, BT, V, w1s, S6, CC, H3, DZ3, LT, dh, acc, d1,
    rsend, r1, r2, f3, r3,
    ab_ss, ab_rs, p_ss, p_rs, f_ss, f_rs, sn_ss, sn_rs, g_ss, g_rs,
    r1_ss, r1_rs, r2_ss, r2_rs, r3_ss, r3_rs,
):
    i = lax.axis_index("gx")
    j = lax.axis_index("gy")
    has_l, has_r = i > 0, i < GX - 1
    has_x = {-1: has_l, 0: True, 1: has_r}
    has_y = {-1: j > 0, 0: True, 1: j < GY - 1}

    def has(d):
        dx, dy = DIRS[d]
        if dx == 0:
            return has_y[dy]
        if dy == 0:
            return has_x[dx]
        return jnp.logical_and(has_x[dx], has_y[dy])

    cy, czh, cc = i // 8, (i // 2) % 4, i % 2
    czl, cx = j // 4, j % 4
    me = cy * 8 + cc * 4 + cx
    mez = czh * 2 + czl

    def member(m):
        return ((m // 8) * 8 + czh * 2 + (m // 4) % 2, czl * 4 + m % 4)

    def zpeer(k):
        return (cy * 8 + (k // 2) * 2 + cc, (k % 2) * 4 + cx)

    bar = pltpu.get_barrier_semaphore()

    def greet(dev):
        pl.semaphore_signal(bar, inc=1, device_id=dev, device_id_type=MESH)

    @pl.when(has_l)
    def _():
        @pl.loop(0, GY)
        def _(s):
            greet((i - 1, s))

    @pl.when(has_r)
    def _():
        @pl.loop(0, GY)
        def _(s):
            greet((i + 1, s))

    @pl.loop(1, GY)
    def _(k):
        greet((i, lax.rem(j + k, GY)))

    @pl.loop(1, GROUP)
    def _(k):
        greet(member(lax.rem(me + k, GROUP)))

    @pl.loop(1, ZS)
    def _(k):
        greet(zpeer(lax.rem(mez + k, ZS)))

    a_own = 1.0 / (6.0 + stf[...])
    b_own = src[...] * a_own
    A[8:16, 8:16, :] = a_own
    B[8:16, 8:16, :] = b_own
    PP[8:16, 8:16, :] = b_own
    absend[...] = jnp.concatenate([a_own, b_own], axis=1).astype(BF16)
    fysend[0] = lev[:, 0, :]
    fysend[1] = lev[:, 7, :]
    zero_tile = jnp.zeros((T, T, FZ), F32)
    for d, (dx, dy) in enumerate(DIRS):
        xs, ys = pl.ds(8 + 8 * dx, 8), pl.ds(8 + 8 * dy, 8)

        @pl.when(jnp.logical_not(has(d)))
        def _():
            A[xs, ys, :] = zero_tile
            B[xs, ys, :] = zero_tile
            PP[xs, ys, :] = zero_tile

    @pl.when(jnp.logical_not(has_l))
    def _():
        fxr[0] = jnp.zeros((T, FZ), F32)
        snrcv[0] = jnp.zeros((GY, 8, 128), F32)
        grcv[0] = jnp.zeros((16, 4096), BF16)

    @pl.when(jnp.logical_not(has_r))
    def _():
        fxr[1] = jnp.zeros((T, FZ), F32)
        snrcv[2] = jnp.zeros((GY, 8, 128), F32)
        grcv[1] = jnp.zeros((16, 4096), BF16)

    @pl.when(j == 0)
    def _():
        fyr[0] = jnp.zeros((T, FZ), F32)

    @pl.when(j == GY - 1)
    def _():
        fyr[1] = jnp.zeros((T, FZ), F32)

    for s in range(1, 8):
        snsend[s] = snp[order[s]]

    n_bar = (GY - 1) + (GROUP - 1) + (ZS - 1)
    n_bar = n_bar + jnp.where(has_l, GY, 0) + jnp.where(has_r, GY, 0)
    pl.semaphore_wait(bar, n_bar)

    def ab_copy(d, to):
        dx, dy = DIRS[d]
        slot = 7 - d if to else d
        send_dx = dx if to else -dx
        rows = {1: pl.ds(T - RAD, RAD), 0: pl.ds(0, T), -1: pl.ds(0, RAD)}[send_dx]
        return pltpu.make_async_remote_copy(
            src_ref=absend.at[rows], dst_ref=abrcv.at[slot, rows],
            send_sem=ab_ss.at[d], recv_sem=ab_rs.at[slot],
            device_id=(i + dx, j + dy), device_id_type=MESH,
        )

    def p_copy(e, d, to):
        dx, dy = DIRS[d]
        slot = 7 - d if to else d
        return pltpu.make_async_remote_copy(
            src_ref=psend.at[e], dst_ref=prcv.at[e, slot],
            send_sem=p_ss.at[e, d], recv_sem=p_rs.at[e, slot],
            device_id=(i + dx, j + dy), device_id_type=MESH,
        )

    def fx_copy(side, to):
        slot = 1 - side if to else side
        return pltpu.make_async_remote_copy(
            src_ref=lev.at[0 if side == 0 else 7], dst_ref=fxr.at[slot],
            send_sem=f_ss.at[side], recv_sem=f_rs.at[slot],
            device_id=(i + (2 * side - 1), j), device_id_type=MESH,
        )

    def fy_copy(side, to):
        slot = 1 - side if to else side
        return pltpu.make_async_remote_copy(
            src_ref=fysend.at[side], dst_ref=fyr.at[slot],
            send_sem=f_ss.at[2 + side], recv_sem=f_rs.at[2 + slot],
            device_id=(i, j + (2 * side - 1)), device_id_type=MESH,
        )

    def g_copy(side, to):
        slot = 1 - side if to else side
        return pltpu.make_async_remote_copy(
            src_ref=g.at[side], dst_ref=grcv.at[slot],
            send_sem=g_ss.at[side], recv_sem=g_rs.at[slot],
            device_id=(i + (2 * side - 1), j), device_id_type=MESH,
        )

    def sn_send(d, s):
        return pltpu.make_async_remote_copy(
            src_ref=snsend.at[s], dst_ref=snrcv.at[1 - d, j],
            send_sem=sn_ss.at[d + 1, s], recv_sem=sn_rs.at[1 - d, j],
            device_id=(i + d, s), device_id_type=MESH,
        )

    def sn_recv(d, y):
        return pltpu.make_async_remote_copy(
            src_ref=snsend.at[0], dst_ref=snrcv.at[d + 1, y],
            send_sem=sn_ss.at[d + 1, 0], recv_sem=sn_rs.at[d + 1, y],
            device_id=(i, j), device_id_type=MESH,
        )

    x_sides = ((0, has_l), (1, has_r))
    y_sides = ((0, has_y[-1]), (1, has_y[1]))

    for d in range(8):
        pl.when(has(d))(lambda d=d: ab_copy(d, True).start())
    for side, ok in x_sides:
        pl.when(ok)(lambda side=side: fx_copy(side, True).start())
    for side, ok in y_sides:
        pl.when(ok)(lambda side=side: fy_copy(side, True).start())
    for side, ok in x_sides:
        pl.when(ok)(lambda side=side: g_copy(side, True).start())

    def each_snap(lo, hi, act):
        @pl.loop(lo, hi)
        def _(s):
            pl.when(has_l)(lambda: act(-1, s))
            pl.when(s != j)(lambda: act(0, s))
            pl.when(has_r)(lambda: act(1, s))

    each_snap(1, GY, lambda d, s: sn_send(d, s).start())

    for a in range(3):
        for b in range(3):
            blk = [
                w2[(9 * a + 3 * b + c) * 64 : (9 * a + 3 * b + c + 1) * 64, :].astype(F32)
                for c in range(3)
            ]
            none = jnp.zeros((64, 64), F32)
            r0 = (b * 2) * 64
            BT[a, r0 : r0 + 64, :] = jnp.concatenate(
                [blk[2], blk[1], blk[0], none], axis=1
            ).astype(BF16)
            BT[a, r0 + 64 : r0 + 128, :] = jnp.concatenate(
                [none, blk[2], blk[1], blk[0]], axis=1
            ).astype(BF16)

    w1s[...] = jnp.zeros((32, 128), F32)
    w1s[0:27, 0:64] = w1[...].astype(F32)
    w1d = w1s[...]
    w1d = jnp.concatenate([w1d, pltpu.roll(w1d, 64, 1)], axis=0).astype(BF16)
    for par in range(2):
        for b in range(3):
            k = iota((256, 64), 0)
            col = iota((256, 64), 1)
            zo = col // 32
            zi = ((k & 63) + 5 - 2 * par) & 3
            cz = zi - zo
            want = 9 * (k // 64) + 3 * b + cz
            hit = (col % 32 == want) & (cz >= 0) & (cz < 3) & (k < 192)
            V[par, :, b * 128 : (b + 1) * 128] = dot(
                jnp.where(hit, 1.0, 0.0).astype(BF16), w1d
            ).astype(BF16)

    lane128 = iota((16, 128), 1)

    def windows(plane, gv):
        gr = pltpu.roll(gv.astype(F32), 64, 1)
        for t in range(33):
            if t == 0:
                tile = jnp.where(lane128 >= 64, gr[:, 0:128], 0.0)
            elif t == 32:
                tile = jnp.where(lane128 < 64, gr[:, 0:128], 0.0)
            else:
                tile = gr[:, 128 * t : 128 * (t + 1)]
            tile = tile.astype(BF16)
            if t < 32:
                r = ((t % 2) * 16 + t // 2) * 16
                W[plane, r : r + 16, 0:128] = tile
            if t > 0:
                r = (((t - 1) % 2) * 16 + (t - 1) // 2) * 16
                W[plane, r : r + 16, 128:256] = tile

    for x in range(2):
        windows(x + 1, g[x])
        GT[x] = W[x + 1].T

    for d, (dx, dy) in enumerate(DIRS):
        lo = {-1: T - RAD, 0: 0, 1: 0}[dx]
        n = T if dx == 0 else RAD
        xs, ys = pl.ds(8 + 8 * dx + lo, n), pl.ds(8 + 8 * dy, 8)

        @pl.when(has(d))
        def _():
            ab_copy(d, False).wait_recv()
            v = abrcv[d, lo : lo + n].astype(F32)
            A[xs, ys, :] = v[:, 0:8]
            B[xs, ys, :] = v[:, 8:16]
            PP[xs, ys, :] = v[:, 8:16]

    def around(v):
        rows = pltpu.roll(v, 1, 0) + pltpu.roll(v, 23, 0)
        return rows + z_before(v, 1) + z_after(v, 1)

    def sweeps(first, count):
        @pl.loop(0, count)
        def _(it):
            rad = first - it
            lo = 8 - rad

            def body(t, carry):
                before, cur = carry
                x = lo + 2 * t
                n1 = PP[x + 1]
                n2 = PP[x + 2]
                PP[x] = B[x] + A[x] * (before + n1 + around(cur))
                PP[x + 1] = B[x + 1] + A[x + 1] * (cur + n2 + around(n1))
                return n1, n2

            lax.fori_loop(0, 4 + rad, body, (PP[lo - 1], PP[lo]))

    def exchange(e, filler):
        own = PP[8:16, 8:16, :]
        psend[e] = own.reshape(4, 16, FZ).astype(BF16)
        for d in range(8):
            pl.when(has(d))(lambda d=d: p_copy(e, d, True).start())
        filler()
        for d, (dx, dy) in enumerate(DIRS):
            xs, ys = pl.ds(8 + 8 * dx, 8), pl.ds(8 + 8 * dy, 8)

            @pl.when(has(d))
            def _():
                p_copy(e, d, False).wait_recv()
                PP[xs, ys, :] = prcv[e, d].astype(F32).reshape(8, 8, FZ)

    def back(x):
        @pl.loop(0, 4)
        def _(q):
            rows = pl.ds(pl.multiple_of(q * 128, 128), 128)
            r = dot(W[x + 2, rows, :], BT[0], ((1,), (1,)))
            r = r + dot(W[x + 1, rows, :], BT[1], ((1,), (1,)))
            r = r + dot(W[x, rows, :], BT[2], ((1,), (1,)))
            dh[x, rows, :] = (
                row_after(r[:, 0:128]) + r[:, 128:256] + row_before(r[:, 256:384])
            )

    def filler_one():
        for side, ok in x_sides:
            pl.when(ok)(lambda side=side: g_copy(side, False).wait_recv())
        windows(0, grcv[0])
        windows(3, grcv[1])
        back(0)

    def filler_two():
        back(1)

    sweeps(RAD - 1, RAD)
    exchange(0, filler_one)
    sweeps(6, 7)
    exchange(1, filler_two)
    sweeps(6, 6)

    for side, ok in x_sides:
        pl.when(ok)(lambda side=side: fx_copy(side, False).wait_recv())
    for side, ok in y_sides:
        pl.when(ok)(lambda side=side: fy_copy(side, False).wait_recv())

    pool = jnp.where(iota((FZ, 128), 0) // 4 == iota((FZ, 128), 1), 1.0 / 64.0, 0.0)
    row8 = iota((8, FZ), 0)
    sums = []
    total = None
    for x in range(8):
        pc = PP[x + 8]
        px = 0.5 * (PP[x + 9, 8:16] - PP[x + 7, 8:16])
        py = 0.5 * (pltpu.roll(pc, 23, 0) - pltpu.roll(pc, 1, 0))[8:16]
        pm = pc[8:16]
        pz = 0.5 * (z_after(pm, 1) - z_before(pm, 1))
        fm = lev[x]
        f_lo = fxr[0] if x == 0 else lev[x - 1]
        f_hi = fxr[1] if x == 7 else lev[x + 1]
        fx = 0.5 * (f_hi - f_lo)
        y_lo = jnp.where(row8 == 0, fyr[0, x : x + 1, :], pltpu.roll(fm, 1, 0))
        y_hi = jnp.where(row8 == 7, fyr[1, x : x + 1, :], pltpu.roll(fm, 7, 0))
        fy = 0.5 * (y_hi - y_lo)
        fz = 0.5 * (z_after(fm, 1) - z_before(fm, 1))
        new = fm + 2.0 * (px * fx + py * fy + pz * fz)
        newl[x] = new
        prs[x] = pm
        total = new if x % 4 == 0 else total + new
        if x % 4 == 3:
            t = total + pltpu.roll(total, 7, 0)
            sums.append(t + pltpu.roll(t, 6, 0))
    mean = dot(jnp.concatenate(sums, axis=0), pool, precision=lax.Precision.HIGHEST)
    for r in range(4):
        snsend[0, r : r + 1, :] = mean[4 * r : 4 * r + 1, :]
    snsend[0, 4:8, :] = jnp.zeros((4, 128), F32)

    each_snap(0, 1, lambda d, s: sn_send(d, s).start())
    snrcv[1, j] = snsend[j]

    @pl.when(has_l)
    def _():
        @pl.loop(0, GY)
        def _(y):
            sn_recv(-1, y).wait_recv()

    @pl.when(has_r)
    def _():
        @pl.loop(0, GY)
        def _(y):
            sn_recv(1, y).wait_recv()

    @pl.loop(1, GY)
    def _(k):
        sn_recv(0, lax.rem(j + k, GY)).wait_recv()

    for d in range(3):
        for y in range(8):
            t = snrcv[d, y]
            S6[2 * d, 2 * y : 2 * y + 2, :] = t[0:2]
            S6[2 * d + 1, 2 * y : 2 * y + 2, :] = t[2:4]
    for p in range(4):
        CC[p, :, 0:128] = S6[p] + pltpu.roll(S6[p + 1], 64, 1)
        CC[p, :, 128:256] = S6[p + 2]

    for p in range(4):
        keep = {0: jnp.where(has_l, 1.0, 0.0), 3: jnp.where(has_r, 1.0, 0.0)}.get(p)

        @pl.loop(0, 4)
        def _(q):
            rows = pl.ds(pl.multiple_of(q * 128, 128), 128)
            par = q // 2
            jj = 2 * ((q % 2) * 8 + iota((8, 16, 256), 0)) + par
            t = (iota((8, 16, 256), 2) & 63) - 2 * jj + 1
            mask = (t >= 0) & (t < 4)
            v = jnp.broadcast_to(CC[p][None], (8, 16, 256))
            v = jnp.where(mask, v, 0.0).reshape(128, 256).astype(BF16)
            r = dot(v, V[par])
            z = row_before(r[:, 0:128]) + r[:, 128:256] + row_after(r[:, 256:384])
            sig = 1.0 / (1.0 + jnp.exp(-z))
            h = z * sig
            if keep is not None:
                h = h * keep
            H3[p, rows, 0:128] = row_before(h).astype(BF16)
            H3[p, rows, 128:256] = h.astype(BF16)
            H3[p, rows, 256:384] = row_after(h).astype(BF16)
            if p in (1, 2):
                dz = dh[p - 1, rows, :] * (sig * (1.0 + z * (1.0 - sig)))
                DZ3[p - 1, rows, 0:128] = row_after(dz).astype(BF16)
                DZ3[p - 1, rows, 128:256] = dz.astype(BF16)
                DZ3[p - 1, rows, 256:384] = row_before(dz).astype(BF16)

    for a in range(3):
        acc[a] = dot(GT[0], H3[a]) + dot(GT[1], H3[a + 1])

    spread = jnp.where((iota((16, ROWS), 1) & 15) == iota((16, ROWS), 0), 1.0, 0.0).astype(BF16)
    r_k = iota((256, ROWS), 0) & 63
    r_c = iota((256, ROWS), 1)
    jj = 2 * ((r_c & 255) // 16) + r_c // 256
    t = r_k - 2 * jj + 1
    near = (t >= 0) & (t < 4)
    for x in range(2):
        LT[x] = jnp.where(near, dot(CC[x + 1].T.astype(BF16), spread), 0.0).astype(BF16)
    parts = []
    for par in range(2):
        cols = slice(par * 256, par * 256 + 256)
        q = dot(LT[0, :, cols], DZ3[0, cols, :]) + dot(LT[1, :, cols], DZ3[1, cols, :])
        q = q.reshape(4, 8, 8, 384)
        parts.append([q[a].sum(0) for a in range(3)])
    d1[...] = jnp.zeros((64, 128), F32)
    for a in range(3):
        u, w = parts[0][a], parts[1][a]
        u = u + pltpu.roll(u, 4, 0)
        w = w + pltpu.roll(w, 4, 0)
        u = u + pltpu.roll(w, 2, 0)
        for b in range(3):
            v = u[:, b * 128 : (b + 1) * 128]
            v = pltpu.roll(v, 64, 1) + pltpu.roll(v, 7, 0)
            v = pltpu.roll(v, 1, 0)
            d1[9 * a + 3 * b : 9 * a + 3 * b + 3, :] = v[0:3]

    lane = iota((64, 128), 1)

    def term(o):
        a, b, c = o // 9, (o // 3) % 3, o % 3
        r = (2 - c) * 64
        cols = slice(b * 128, b * 128 + 128)
        v = jnp.where(lane < 64, acc[a, r : r + 64, cols], acc[a, r + 64 : r + 128, cols])
        return v + pltpu.roll(v, 64, 1)

    for q in range(14):
        other = term(2 * q + 1) if q < 13 else d1[...]
        v = jnp.where(lane < 64, term(2 * q), other)
        rsend[2 * q] = v[0:32].astype(BF16)
        rsend[2 * q + 1] = v[32:64].astype(BF16)

    def r1_send(m):
        return pltpu.make_async_remote_copy(
            src_ref=rsend.at[m], dst_ref=r1.at[me],
            send_sem=r1_ss.at[m], recv_sem=r1_rs.at[me],
            device_id=member(m), device_id_type=MESH,
        )

    def r1_recv(m):
        return pltpu.make_async_remote_copy(
            src_ref=rsend.at[0], dst_ref=r1.at[m],
            send_sem=r1_ss.at[0], recv_sem=r1_rs.at[m],
            device_id=member(m), device_id_type=MESH,
        )

    def r2_copy(k, slot):
        return pltpu.make_async_remote_copy(
            src_ref=r2.at[mez], dst_ref=r2.at[slot],
            send_sem=r2_ss.at[k], recv_sem=r2_rs.at[slot],
            device_id=zpeer(k), device_id_type=MESH,
        )

    def r3_copy(m, slot):
        return pltpu.make_async_remote_copy(
            src_ref=f3, dst_ref=r3.at[slot],
            send_sem=r3_ss.at[m], recv_sem=r3_rs.at[slot],
            device_id=member(m), device_id_type=MESH,
        )

    @pl.loop(1, GROUP)
    def _(k):
        m = lax.rem(me + k, GROUP)
        pl.when(m < CHUNKS)(lambda: r1_send(m).start())

    @pl.when(me < CHUNKS)
    def _():
        def add(k, total):
            m = lax.rem(me + k, GROUP)
            r1_recv(m).wait_recv()
            return total + r1[m].astype(F32)

        r2[mez] = lax.fori_loop(1, GROUP, add, rsend[me].astype(F32))

        @pl.loop(1, ZS)
        def _(k):
            r2_copy(lax.rem(mez + k, ZS), mez).start()

        @pl.loop(1, ZS)
        def _(k):
            m = lax.rem(mez + k, ZS)
            r2_copy(m, m).wait_recv()

        total = r2[0]
        for k in range(1, ZS):
            total = total + r2[k]
        f3[...] = total.astype(BF16)

        @pl.loop(1, GROUP)
        def _(k):
            r3_copy(lax.rem(me + k, GROUP), me).start()

        r3[me] = f3[...]

    @pl.loop(1, GROUP)
    def _(k):
        m = lax.rem(me + k, GROUP)
        pl.when(m < CHUNKS)(lambda: r3_copy(m, m).wait_recv())

    for q in range(14):
        v = jnp.concatenate([r3[2 * q], r3[2 * q + 1]], axis=0).astype(F32)
        vt = v.T
        if q < 13:
            dw2o[128 * q : 128 * q + 128, :] = vt
        else:
            dw2o[128 * q : 128 * q + 64, :] = vt[0:64]
            dw1o[...] = pltpu.roll(v, 64, 1)[0:27, 0:64]

    for d in range(8):
        @pl.when(has(d))
        def _():
            ab_copy(d, True).wait_send()
            p_copy(0, d, True).wait_send()
            p_copy(1, d, True).wait_send()

    for side, ok in x_sides:
        @pl.when(ok)
        def _():
            fx_copy(side, True).wait_send()
            g_copy(side, True).wait_send()

    for side, ok in y_sides:
        pl.when(ok)(lambda side=side: fy_copy(side, True).wait_send())
    each_snap(0, GY, lambda d, s: sn_send(d, s).wait_send())

    @pl.loop(1, GROUP)
    def _(k):
        m = lax.rem(me + k, GROUP)
        pl.when(m < CHUNKS)(lambda: r1_send(m).wait_send())
        pl.when(me < CHUNKS)(lambda: r3_copy(m, me).wait_send())

    @pl.when(me < CHUNKS)
    def _():
        @pl.loop(1, ZS)
        def _(k):
            r2_copy(lax.rem(mez + k, ZS), mez).wait_send()


def per_device(
    level_set, source, stiffness, snap_buffer, buffer_order, first_weight, second_weight, out_grad
):
    snap = jnp.pad(
        snap_buffer.reshape(8, 4, 64).astype(F32), ((0, 0), (0, 4), (0, 64))
    )
    g = out_grad.reshape(2, 16, 4096)
    vm = pl.BlockSpec(memory_space=pltpu.VMEM)
    sm = pl.BlockSpec(memory_space=pltpu.SMEM)
    dma = pltpu.SemaphoreType.DMA
    return pl.pallas_call(
        kernel,
        out_shape=(
            jax.ShapeDtypeStruct((8, 8, FZ), F32),
            jax.ShapeDtypeStruct((8, 8, FZ), F32),
            jax.ShapeDtypeStruct((27, 64), F32),
            jax.ShapeDtypeStruct((1728, 64), F32),
        ),
        in_specs=[vm, vm, vm, vm, sm, vm, vm, vm],
        out_specs=(vm, vm, vm, vm),
        scratch_shapes=[
            pltpu.VMEM((24, 24, FZ), F32),
            pltpu.VMEM((24, 24, FZ), F32),
            pltpu.VMEM((24, 24, FZ), F32),
            pltpu.VMEM((8, 16, FZ), BF16),
            pltpu.VMEM((8, 8, 16, FZ), BF16),
            pltpu.VMEM((2, 4, 16, FZ), BF16),
            pltpu.VMEM((2, 8, 4, 16, FZ), BF16),
            pltpu.VMEM((2, 8, FZ), F32),
            pltpu.VMEM((2, 8, FZ), F32),
            pltpu.VMEM((2, 8, FZ), F32),
            pltpu.VMEM((8, 8, 128), F32),
            pltpu.VMEM((3, 8, 8, 128), F32),
            pltpu.VMEM((2, 16, 4096), BF16),
            pltpu.VMEM((4, ROWS, 256), BF16),
            pltpu.VMEM((2, 256, ROWS), BF16),
            pltpu.VMEM((3, 384, 256), BF16),
            pltpu.VMEM((2, 256, 384), BF16),
            pltpu.VMEM((32, 128), F32),
            pltpu.VMEM((6, 16, 128), F32),
            pltpu.VMEM((4, 16, 256), F32),
            pltpu.VMEM((4, ROWS, 384), BF16),
            pltpu.VMEM((2, ROWS, 384), BF16),
            pltpu.VMEM((2, 256, ROWS), BF16),
            pltpu.VMEM((2, ROWS, 128), F32),
            pltpu.VMEM((3, 256, 384), F32),
            pltpu.VMEM((64, 128), F32),
            pltpu.VMEM((CHUNKS, 32, 128), BF16),
            pltpu.VMEM((GROUP, 32, 128), BF16),
            pltpu.VMEM((ZS, 32, 128), F32),
            pltpu.VMEM((32, 128), BF16),
            pltpu.VMEM((CHUNKS, 32, 128), BF16),
            dma((8,)), dma((8,)), dma((2, 8)), dma((2, 8)), dma((4,)), dma((4,)),
            dma((3, 8)), dma((3, 8)), dma((2,)), dma((2,)),
            dma((CHUNKS,)), dma((GROUP,)), dma((ZS,)), dma((ZS,)), dma((GROUP,)), dma((CHUNKS,)),
        ],
        compiler_params=pltpu.CompilerParams(
            collective_id=0, has_side_effects=True, vmem_limit_bytes=48 * 1024 * 1024
        ),
    )(source, stiffness, level_set, snap, buffer_order, first_weight, second_weight, g)


def solution(mesh):
    placed = (
        P("gx", "gy", None),
        P("gx", "gy", None),
        P("gx", "gy", None),
        P(None, "gx", "gy", None),
        P(),
        P(),
        P(),
        P("gy", "gx", None, None),
    )
    return jax.shard_map(
        per_device,
        mesh=mesh,
        in_specs=placed,
        out_specs=(P("gx", "gy", None), P("gx", "gy", None), P(), P()),
        check_vma=False,
    )
```

time: 804 us -> 84.6 us (0.11)
  starting transfers between devices: 398 us -> 0 us
  waiting for transfers between devices: 206 us -> 0 us
  blocking collectives: 98.5 us -> 0 us
  Pallas kernels: 0 us -> 78.9 us
  other arithmetic: 38 us -> 0.7 us
  local copies, waits for them, and re-layouts: 31.3 us -> 4.2 us
  between operations: 15.1 us -> 0.72 us
  matrix products: 10.3 us -> 0 us
    ppermute x94 -> x0, starting transfers between devices: 385 us -> none  [the longest x47 308 us: padded_2(): lax.ppermute(lax.slice_in_dim(block, block.shape[dim] - width, None, axis...]
    psum x1 -> x0, waiting for transfers between devices: 170 us -> none  [per_device(): dw_first, dw_second = lax.psum((dw_one, dw_two), ('gx', 'gy'))]
    psum x1 -> x0, blocking collectives: 98.5 us -> none  [per_device(): dw_first, dw_second = lax.psum((dw_one, dw_two), ('gx', 'gy'))]
    pallas_call x0 -> x1, Pallas kernels: none -> 78.9 us  [per_device(): pl.pallas_call(kernel, out_shape=(jax.ShapeDtypeStruct((8, 8, FZ), F32),...]
    ppermute x94 -> x0, waiting for transfers between devices: 31.6 us -> none  [the longest x47 31.5 us: padded_2(): lax.ppermute(lax.slice_in_dim(block, block.shape[dim] - width, None, axis...]
    div x20 -> x0, other arithmetic: 19.4 us -> none  [sweep(): return (source + neighbours(tile_faces(press))) / (6.0 + stiffness)]
    concatenate x55 -> x0, other arithmetic: 17.8 us -> none  [the longest x46 6.26 us: padded_2(): block = jnp.concatenate([low, block, high], axis=dim)]
    all_to_all x1 -> x0, starting transfers between devices: 13.4 us -> none  [per_device(): lax.all_to_all(local_snaps, 'gy', split_axis=0, concat_axis=2, tiled=True)]
  transfers between devices with their start and end apart: 96 -> 0, of which waited for: 43 -> 0; matrix products, arithmetic and copies ran while one was open for 7% -> 0% of each run, Pallas kernels for 0% -> 0%
where the time goes in v1:
time: 84.6 us; the launch traced here: 84.5 us
  Pallas kernels  78.9 us (93%)
  local copies, waits for them, and re-layouts  4.2 us (5%)
    pallas_call x1, Pallas kernels, per_device(): pl.pallas_call(kernel, out_shape=(jax.ShapeDtypeStruct((8, 8, FZ), F32),...  78.9 us
    unnamed x16, local copies, waits for them, and re-layouts  3.15 us

profile of v1, /device:TPU:1, one launch (start us, length us, event | category | flops | bytes accessed | tf_op | source)
XLA Modules:
  0.0 84.5 jit_solution(7809362807143613553)
XLA Ops:
  0.6 0.7 pad_convert_fusion.snp
  1.3 0.0 copy-start
  1.3 0.0 copy-start.1
  1.3 0.0 copy-start.2
  1.4 0.0 copy-start.3
  1.4 0.0 copy-start.4
  1.4 0.0 copy-start.5
  1.4 1.2 %copy.12.w2 = bf16[1728,64]{1,0:T(8,128)(2,1)S(1)} copy(bf16[1728,64]{0,1:T(8,128)(2,1)} %param.14) | data formatting | bytes 442368 | tf_op args[6]
  2.6 0.0 copy-done
  2.6 0.0 copy-done.1
  2.7 0.0 copy-done.2
  2.7 0.0 copy-done.3
  2.7 0.0 copy-done.4
  2.7 0.0 copy-done.5
  2.7 78.9 %shard_map.111 = (f32[8,8,256]{2,1,0:T(8,128)S(1)}, f32[8,8,256]{2,1,0:T(8,128)S(1)}, f32[27,64]{1,0:T(8,128)S(1)}, f32[1728,64]{1,0:T(8,128)S(1)}) custom-call(f32[8,8,256]{2,1,0:T(8,128)S(1)} %copy-done.1, f32[8,8,256]{2,1,0:T(8,128)S(1)} %copy-done.2, f32[8,8,256]{2,1,0:T(8,128)S(1)} %copy-done.3, f32[8,8,128]{2,1,0:T(8,128)S(1)} %pad_convert_fusion.snp, ...), custom_call_target="tpu_custom_call" | custom-call | tf_op jit(solution)/shard_map/pallas_call | solution.py:621
  81.6 1.1 %copy.13 = f32[1728,64]{0,1:T(8,128)} copy(f32[1728,64]{1,0:T(8,128)S(1)} %get-tuple-element.7) | data formatting | bytes 884736 | tf_op jit(solution)/shard_map/pallas_call | solution.py:621
  82.6 0.6 copy.17
  83.3 0.6 copy.18
  83.9 0.6 copy.19
Async XLA Ops:
  1.3 1.3 %copy-start = (bf16[1,2,16,4096]{3,2,1,0:T(8,128)(2,1)S(1)}, bf16[1,2,16,4096]{3,2,1,0:T(8,128)(2,1)}, u32[]{:S(2)}) copy-start(bf16[1,2,16,4096]{3,2,1,0:T(8,128)(2,1)} %param.15) | copy-start | bytes 786436
  1.3 1.3 %copy-start.1 = (f32[8,8,256]{2,1,0:T(8,128)S(1)}, f32[8,8,256]{2,1,0:T(8,128)}, u32[]{:S(2)}) copy-start(f32[8,8,256]{2,1,0:T(8,128)} %src.1) | copy-start | bytes 196612
  1.3 1.3 %copy-start.2 = (f32[8,8,256]{2,1,0:T(8,128)S(1)}, f32[8,8,256]{2,1,0:T(8,128)}, u32[]{:S(2)}) copy-start(f32[8,8,256]{2,1,0:T(8,128)} %stf.1) | copy-start | bytes 196612
  1.4 1.3 %copy-start.3 = (f32[8,8,256]{2,1,0:T(8,128)S(1)}, f32[8,8,256]{2,1,0:T(8,128)}, u32[]{:S(2)}) copy-start(f32[8,8,256]{2,1,0:T(8,128)} %lev.1) | copy-start | bytes 196612
  1.4 1.3 %copy-start.4 = (bf16[27,64]{1,0:T(8,128)(2,1)S(1)}, bf16[27,64]{1,0:T(8,128)(2,1)}, u32[]{:S(2)}) copy-start(bf16[27,64]{1,0:T(8,128)(2,1)} %w1.1) | copy-start | bytes 10372
  1.4 1.3 %copy-start.5 = (s32[8]{0:T(128)S(1)}, s32[8]{0:T(128)}, u32[]{:S(2)}) copy-start(s32[8]{0:T(128)} %order.1) | copy-start | bytes 100

commit v2 on v1

--- a/solution.py
+++ b/solution.py
@@ -31,6 +31,10 @@
     return lax.broadcasted_iota(jnp.int32, shape, dim)
 
 
+def tile_rows(dx, n):
+    return {-1: (T - n, n), 0: (0, T), 1: (0, n)}[dx]
+
+
 def row_before(v):
     y = iota(v.shape, 0) & 15
     return jnp.where(y == 0, 0.0, pltpu.roll(v, 1, 0))
@@ -52,8 +56,10 @@
 
 
 def kernel(
-    src, stf, lev, snp, order, w1, w2, g,
-    newl, prs, dw1o, dw2o,
+    src_h, stf_h, lev_h, snp, order, w1, w2_h, g_h,
+    newl_h, prs_h, dw1_h, dw2_h,
+    newl, prs, dw1o, dw2o, out_s,
+    src, stf, lev, w2, g, w2p, in_s,
     A, B, PP, absend, abrcv, psend, prcv, fysend, fxr, fyr,
     snsend, snrcv, grcv, W, GT, BT, V, w1s, S6, CC, H3, DZ3, LT, dh, acc, d1,
     rsend, r1, r2, f3, r3,
@@ -85,6 +91,15 @@
     def zpeer(k):
         return (cy * 8 + (k // 2) * 2 + cc, (k % 2) * 4 + cx)
 
+    loads = [
+        pltpu.make_async_copy(a, b, in_s.at[k])
+        for k, (a, b) in enumerate(
+            ((src_h, src), (stf_h, stf), (lev_h, lev), (g_h, g), (w2_h, w2))
+        )
+    ]
+    for c in loads:
+        c.start()
+
     bar = pltpu.get_barrier_semaphore()
 
     def greet(dev):
@@ -114,6 +129,8 @@
     def _(k):
         greet(zpeer(lax.rem(mez + k, ZS)))
 
+    for c in loads[:4]:
+        c.wait()
     a_own = 1.0 / (6.0 + stf[...])
     b_own = src[...] * a_own
     A[8:16, 8:16, :] = a_own
@@ -152,8 +169,9 @@
     def _():
         fyr[1] = jnp.zeros((T, FZ), F32)
 
+    snsend[...] = jnp.zeros((8, 8, 128), F32)
     for s in range(1, 8):
-        snsend[s] = snp[order[s]]
+        snsend[s, 0:4, 0:64] = snp[order[s]].astype(F32)
 
     n_bar = (GY - 1) + (GROUP - 1) + (ZS - 1)
     n_bar = n_bar + jnp.where(has_l, GY, 0) + jnp.where(has_r, GY, 0)
@@ -163,7 +181,8 @@
         dx, dy = DIRS[d]
         slot = 7 - d if to else d
         send_dx = dx if to else -dx
-        rows = {1: pl.ds(T - RAD, RAD), 0: pl.ds(0, T), -1: pl.ds(0, RAD)}[send_dx]
+        lo, n = tile_rows(-send_dx, RAD if dy == 0 else RAD - 1)
+        rows = pl.ds(lo, n)
         return pltpu.make_async_remote_copy(
             src_ref=absend.at[rows], dst_ref=abrcv.at[slot, rows],
             send_sem=ab_ss.at[d], recv_sem=ab_rs.at[slot],
@@ -173,8 +192,10 @@
     def p_copy(e, d, to):
         dx, dy = DIRS[d]
         slot = 7 - d if to else d
-        return pltpu.make_async_remote_copy(
-            src_ref=psend.at[e], dst_ref=prcv.at[e, slot],
+        lo, n = tile_rows(-dx if to else dx, 8 if dy == 0 else 6)
+        rows = pl.ds(lo // 2, n // 2)
+        return pltpu.make_async_remote_copy(
+            src_ref=psend.at[e, rows], dst_ref=prcv.at[e, slot, rows],
             send_sem=p_ss.at[e, d], recv_sem=p_rs.at[e, slot],
             device_id=(i + dx, j + dy), device_id_type=MESH,
         )
@@ -238,20 +259,27 @@
 
     each_snap(1, GY, lambda d, s: sn_send(d, s).start())
 
+    loads[4].wait()
+    w2p[:, 0:1728] = w2[...].astype(F32)
+    even = w2p[...]
+    odd = pltpu.roll(even, 64, 1)
+    left = iota((64, 128), 1) < 64
+
+    def pair(o):
+        t = ((o + 1) // 2) * 128
+        return (odd if o % 2 else even)[:, t : t + 128]
+
     for a in range(3):
         for b in range(3):
-            blk = [
-                w2[(9 * a + 3 * b + c) * 64 : (9 * a + 3 * b + c + 1) * 64, :].astype(F32)
-                for c in range(3)
-            ]
-            none = jnp.zeros((64, 64), F32)
-            r0 = (b * 2) * 64
-            BT[a, r0 : r0 + 64, :] = jnp.concatenate(
-                [blk[2], blk[1], blk[0], none], axis=1
-            ).astype(BF16)
-            BT[a, r0 + 64 : r0 + 128, :] = jnp.concatenate(
-                [none, blk[2], blk[1], blk[0]], axis=1
-            ).astype(BF16)
+            o = 9 * a + 3 * b
+            tiles = (
+                jnp.where(left, pair(o + 2), 0.0),
+                pair(o + 1),
+                pair(o),
+                jnp.where(left, 0.0, pair(o - 1)),
+            )
+            for k, v in enumerate(tiles):
+                BT[a, 64 * k : 64 * k + 64, 128 * b : 128 * b + 128] = v.astype(BF16)
 
     w1s[...] = jnp.zeros((32, 128), F32)
     w1s[0:27, 0:64] = w1[...].astype(F32)
@@ -294,8 +322,7 @@
         GT[x] = W[x + 1].T
 
     for d, (dx, dy) in enumerate(DIRS):
-        lo = {-1: T - RAD, 0: 0, 1: 0}[dx]
-        n = T if dx == 0 else RAD
+        lo, n = tile_rows(dx, RAD if dy == 0 else RAD - 1)
         xs, ys = pl.ds(8 + 8 * dx + lo, n), pl.ds(8 + 8 * dy, 8)
 
         @pl.when(has(d))
@@ -311,21 +338,13 @@
         return rows + z_before(v, 1) + z_after(v, 1)
 
     def sweeps(first, count):
-        @pl.loop(0, count)
-        def _(it):
-            rad = first - it
-            lo = 8 - rad
-
-            def body(t, carry):
-                before, cur = carry
-                x = lo + 2 * t
-                n1 = PP[x + 1]
-                n2 = PP[x + 2]
-                PP[x] = B[x] + A[x] * (before + n1 + around(cur))
-                PP[x + 1] = B[x + 1] + A[x + 1] * (cur + n2 + around(n1))
-                return n1, n2
-
-            lax.fori_loop(0, 4 + rad, body, (PP[lo - 1], PP[lo]))
+        for rad in range(first, first - count, -1):
+            lo, hi = 8 - rad, 16 + rad
+            before, cur = PP[lo - 1], PP[lo]
+            for x in range(lo, hi):
+                after = PP[x + 1]
+                PP[x] = B[x] + A[x] * (before + after + around(cur))
+                before, cur = cur, after
 
     def exchange(e, filler):
         own = PP[8:16, 8:16, :]
@@ -334,20 +353,22 @@
             pl.when(has(d))(lambda d=d: p_copy(e, d, True).start())
         filler()
         for d, (dx, dy) in enumerate(DIRS):
-            xs, ys = pl.ds(8 + 8 * dx, 8), pl.ds(8 + 8 * dy, 8)
+            lo, n = tile_rows(dx, 8 if dy == 0 else 6)
+            xs, ys = pl.ds(8 + 8 * dx + lo, n), pl.ds(8 + 8 * dy, 8)
 
             @pl.when(has(d))
             def _():
                 p_copy(e, d, False).wait_recv()
-                PP[xs, ys, :] = prcv[e, d].astype(F32).reshape(8, 8, FZ)
+                v = prcv[e, d, lo // 2 : (lo + n) // 2].astype(F32)
+                PP[xs, ys, :] = v.reshape(n, 8, FZ)
 
     def back(x):
         @pl.loop(0, 4)
         def _(q):
             rows = pl.ds(pl.multiple_of(q * 128, 128), 128)
-            r = dot(W[x + 2, rows, :], BT[0], ((1,), (1,)))
-            r = r + dot(W[x + 1, rows, :], BT[1], ((1,), (1,)))
-            r = r + dot(W[x, rows, :], BT[2], ((1,), (1,)))
+            r = dot(W[x + 2, rows, :], BT[0])
+            r = r + dot(W[x + 1, rows, :], BT[1])
+            r = r + dot(W[x, rows, :], BT[2])
             dh[x, rows, :] = (
                 row_after(r[:, 0:128]) + r[:, 128:256] + row_before(r[:, 256:384])
             )
@@ -404,6 +425,14 @@
     snsend[0, 4:8, :] = jnp.zeros((4, 128), F32)
 
     each_snap(0, 1, lambda d, s: sn_send(d, s).start())
+    stores = [
+        pltpu.make_async_copy(a, b, out_s.at[k])
+        for k, (a, b) in enumerate(
+            ((newl, newl_h), (prs, prs_h), (dw1o, dw1_h), (dw2o, dw2_h))
+        )
+    ]
+    stores[0].start()
+    stores[1].start()
     snrcv[1, j] = snsend[j]
 
     @pl.when(has_l)
@@ -434,9 +463,8 @@
     for p in range(4):
         keep = {0: jnp.where(has_l, 1.0, 0.0), 3: jnp.where(has_r, 1.0, 0.0)}.get(p)
 
-        @pl.loop(0, 4)
-        def _(q):
-            rows = pl.ds(pl.multiple_of(q * 128, 128), 128)
+        for q in range(4):
+            rows = slice(q * 128, q * 128 + 128)
             par = q // 2
             jj = 2 * ((q % 2) * 8 + iota((8, 16, 256), 0)) + par
             t = (iota((8, 16, 256), 2) & 63) - 2 * jj + 1
@@ -571,12 +599,14 @@
 
     for q in range(14):
         v = jnp.concatenate([r3[2 * q], r3[2 * q + 1]], axis=0).astype(F32)
-        vt = v.T
         if q < 13:
-            dw2o[128 * q : 128 * q + 128, :] = vt
+            dw2o[:, 128 * q : 128 * q + 128] = v
         else:
-            dw2o[128 * q : 128 * q + 64, :] = vt[0:64]
+            dw2o[:, 128 * q : 128 * q + 64] = v[:, 0:64]
             dw1o[...] = pltpu.roll(v, 64, 1)[0:27, 0:64]
+
+    stores[2].start()
+    stores[3].start()
 
     for d in range(8):
         @pl.when(has(d))
@@ -607,28 +637,43 @@
         def _(k):
             r2_copy(lax.rem(mez + k, ZS), mez).wait_send()
 
+    for c in stores:
+        c.wait()
+
 
 def per_device(
     level_set, source, stiffness, snap_buffer, buffer_order, first_weight, second_weight, out_grad
 ):
-    snap = jnp.pad(
-        snap_buffer.reshape(8, 4, 64).astype(F32), ((0, 0), (0, 4), (0, 64))
-    )
+    snap = snap_buffer.reshape(8, 4, 64)
     g = out_grad.reshape(2, 16, 4096)
     vm = pl.BlockSpec(memory_space=pltpu.VMEM)
     sm = pl.BlockSpec(memory_space=pltpu.SMEM)
+    hbm = pl.BlockSpec(memory_space=pltpu.HBM)
     dma = pltpu.SemaphoreType.DMA
-    return pl.pallas_call(
+    shapes = (
+        jax.ShapeDtypeStruct((8, 8, FZ), F32),
+        jax.ShapeDtypeStruct((8, 8, FZ), F32),
+        jax.ShapeDtypeStruct((27, 64), F32),
+        jax.ShapeDtypeStruct((64, 1728), F32),
+    )
+    results = pl.pallas_call(
         kernel,
-        out_shape=(
-            jax.ShapeDtypeStruct((8, 8, FZ), F32),
-            jax.ShapeDtypeStruct((8, 8, FZ), F32),
-            jax.ShapeDtypeStruct((27, 64), F32),
-            jax.ShapeDtypeStruct((1728, 64), F32),
-        ),
-        in_specs=[vm, vm, vm, vm, sm, vm, vm, vm],
-        out_specs=(vm, vm, vm, vm),
+        out_shape=shapes,
+        in_specs=[hbm, hbm, hbm, vm, sm, vm, hbm, hbm],
+        out_specs=(hbm,) * 4,
         scratch_shapes=[
+            pltpu.VMEM((8, 8, FZ), F32),
+            pltpu.VMEM((8, 8, FZ), F32),
+            pltpu.VMEM((27, 64), F32),
+            pltpu.VMEM((64, 1728), F32),
+            dma((4,)),
+            pltpu.VMEM((8, 8, FZ), F32),
+            pltpu.VMEM((8, 8, FZ), F32),
+            pltpu.VMEM((8, 8, FZ), F32),
+            pltpu.VMEM((64, 1728), BF16),
+            pltpu.VMEM((2, 16, 4096), BF16),
+            pltpu.VMEM((64, 1792), F32),
+            dma((5,)),
             pltpu.VMEM((24, 24, FZ), F32),
             pltpu.VMEM((24, 24, FZ), F32),
             pltpu.VMEM((24, 24, FZ), F32),
@@ -644,7 +689,7 @@
             pltpu.VMEM((2, 16, 4096), BF16),
             pltpu.VMEM((4, ROWS, 256), BF16),
             pltpu.VMEM((2, 256, ROWS), BF16),
-            pltpu.VMEM((3, 384, 256), BF16),
+            pltpu.VMEM((3, 256, 384), BF16),
             pltpu.VMEM((2, 256, 384), BF16),
             pltpu.VMEM((32, 128), F32),
             pltpu.VMEM((6, 16, 128), F32),
@@ -665,9 +710,10 @@
             dma((CHUNKS,)), dma((GROUP,)), dma((ZS,)), dma((ZS,)), dma((GROUP,)), dma((CHUNKS,)),
         ],
         compiler_params=pltpu.CompilerParams(
-            collective_id=0, has_side_effects=True, vmem_limit_bytes=48 * 1024 * 1024
+            collective_id=0, has_side_effects=True, vmem_limit_bytes=60 * 1024 * 1024
         ),
-    )(source, stiffness, level_set, snap, buffer_order, first_weight, second_weight, g)
+    )(source, stiffness, level_set, snap, buffer_order, first_weight, second_weight.T, g)
+    return results[0], results[1], results[2], results[3].T
 
 
 def solution(mesh):

time: 84.6 us -> 71.6 us (0.85)
  Pallas kernels: 78.9 us -> 66.1 us
    pallas_call x1, Pallas kernels: 78.9 us -> 66.1 us  [per_device(): pl.pallas_call(kernel, out_shape=shapes, in_specs=[hbm, hbm, hbm, vm, sm,...]
    unnamed x16 -> x8, local copies, waits for them, and re-layouts: 3.15 us -> 4.64 us
    pallas_call x1 -> x0, local copies, waits for them, and re-layouts: 1.05 us -> none  [per_device(): pl.pallas_call(kernel, out_shape=(jax.ShapeDtypeStruct((8, 8, FZ), F32),...]
where the time goes in v2:
time: 71.6 us; the launch traced here: 71.4 us
  Pallas kernels  66.1 us (92%)
  local copies, waits for them, and re-layouts  4.64 us (6%)
    pallas_call x1, Pallas kernels, per_device(): pl.pallas_call(kernel, out_shape=shapes, in_specs=[hbm, hbm, hbm, vm, sm,...  66.1 us
    unnamed x8, local copies, waits for them, and re-layouts  4.64 us

profile of v2, /device:TPU:1, one launch (start us, length us, event | category | flops | bytes accessed | tf_op | source)
XLA Modules:
  0.0 71.4 jit_solution(8419216022523862287)
XLA Ops:
  0.6 66.1 %shard_map.111 = (f32[8,8,256]{2,1,0:T(8,128)}, f32[8,8,256]{2,1,0:T(8,128)}, f32[27,64]{1,0:T(8,128)}, f32[64,1728]{1,0:T(8,128)}) custom-call(f32[8,8,256]{2,1,0:T(8,128)} %src_h.1, f32[8,8,256]{2,1,0:T(8,128)} %stf_h.1, f32[8,8,256]{2,1,0:T(8,128)} %lev_h.1, bf16[8,4,64]{2,1,0:T(4,128)(2,1)} %bitcast.7, s32[8]{0:T(128)} %order.1, bf16[27,64]{1,0:T(8,128)(2,1)} %w1.1, ...), custom_call_target="tpu_custom_call" | custom-call | tf_op jit(solution)/shard_map/pallas_call | solution.py:659
  66.7 0.0 copy-start
  66.7 1.5 %copy.16 = f32[8,8,256]{2,1,0:T(8,128)} copy(f32[8,8,256]{2,1,0:T(8,128)} %get-tuple-element.16) | data formatting | bytes 131072
  68.2 0.0 copy-done
  68.2 0.0 copy-start.1
  68.2 0.6 copy.17
  68.9 0.1 copy-done.1
  68.9 0.6 copy.18
  69.5 1.8 %copy.19 = f32[1728,64]{0,1:T(8,128)} copy(f32[1728,64]{0,1:T(8,128)} %bitcast.4) | data formatting | bytes 884736
Async XLA Ops:
  66.7 1.5 %copy-start = (f32[8,8,256]{2,1,0:T(8,128)S(1)}, f32[8,8,256]{2,1,0:T(8,128)}, u32[]{:S(2)}) copy-start(f32[8,8,256]{2,1,0:T(8,128)} %get-tuple-element.17) | copy-start | bytes 196612
  68.2 0.7 %copy-start.1 = (f32[27,64]{1,0:T(8,128)S(1)}, f32[27,64]{1,0:T(8,128)}, u32[]{:S(2)}) copy-start(f32[27,64]{1,0:T(8,128)} %get-tuple-element.18) | copy-start | bytes 20740

commit v3 on v2

--- a/solution.py
+++ b/solution.py
@@ -57,8 +57,8 @@
 
 def kernel(
     src_h, stf_h, lev_h, snp, order, w1, w2_h, g_h,
-    newl_h, prs_h, dw1_h, dw2_h,
-    newl, prs, dw1o, dw2o, out_s,
+    newl_h, prs_h, sum_h,
+    newl, prs, out_s,
     src, stf, lev, w2, g, w2p, in_s,
     A, B, PP, absend, abrcv, psend, prcv, fysend, fxr, fyr,
     snsend, snrcv, grcv, W, GT, BT, V, w1s, S6, CC, H3, DZ3, LT, dh, acc, d1,
@@ -373,15 +373,149 @@
                 row_after(r[:, 0:128]) + r[:, 128:256] + row_before(r[:, 256:384])
             )
 
+    lane = iota((64, 128), 1)
+
+    def term(o):
+        a, b, c = o // 9, (o // 3) % 3, o % 3
+        r = (2 - c) * 64
+        cols = slice(b * 128, b * 128 + 128)
+        v = jnp.where(lane < 64, acc[a, r : r + 64, cols], acc[a, r + 64 : r + 128, cols])
+        return v + pltpu.roll(v, 64, 1)
+
+    def r1_send(m):
+        return pltpu.make_async_remote_copy(
+            src_ref=rsend.at[m], dst_ref=r1.at[me],
+            send_sem=r1_ss.at[m], recv_sem=r1_rs.at[me],
+            device_id=member(m), device_id_type=MESH,
+        )
+
+    def r1_recv(m):
+        return pltpu.make_async_remote_copy(
+            src_ref=rsend.at[0], dst_ref=r1.at[m],
+            send_sem=r1_ss.at[0], recv_sem=r1_rs.at[m],
+            device_id=member(m), device_id_type=MESH,
+        )
+
+    def r2_copy(k, slot):
+        return pltpu.make_async_remote_copy(
+            src_ref=r2.at[mez], dst_ref=r2.at[slot],
+            send_sem=r2_ss.at[k], recv_sem=r2_rs.at[slot],
+            device_id=zpeer(k), device_id_type=MESH,
+        )
+
+    def r3_copy(m, slot):
+        return pltpu.make_async_remote_copy(
+            src_ref=f3, dst_ref=r3.at[slot],
+            send_sem=r3_ss.at[m], recv_sem=r3_rs.at[slot],
+            device_id=member(m), device_id_type=MESH,
+        )
+
+    def first_gradient():
+        spread = jnp.where((iota((16, ROWS), 1) & 15) == iota((16, ROWS), 0), 1.0, 0.0).astype(BF16)
+        r_k = iota((256, ROWS), 0) & 63
+        r_c = iota((256, ROWS), 1)
+        jj = 2 * ((r_c & 255) // 16) + r_c // 256
+        t = r_k - 2 * jj + 1
+        near = (t >= 0) & (t < 4)
+        for x in range(2):
+            LT[x] = jnp.where(near, dot(CC[x + 1].T.astype(BF16), spread), 0.0).astype(BF16)
+        parts = []
+        for par in range(2):
+            cols = slice(par * 256, par * 256 + 256)
+            q = dot(LT[0, :, cols], DZ3[0, cols, :]) + dot(LT[1, :, cols], DZ3[1, cols, :])
+            q = q.reshape(4, 8, 8, 384)
+            parts.append([q[a].sum(0) for a in range(3)])
+        d1[...] = jnp.zeros((64, 128), F32)
+        for a in range(3):
+            u, w = parts[0][a], parts[1][a]
+            u = u + pltpu.roll(u, 4, 0)
+            w = w + pltpu.roll(w, 4, 0)
+            u = u + pltpu.roll(w, 2, 0)
+            for b in range(3):
+                v = u[:, b * 128 : (b + 1) * 128]
+                v = pltpu.roll(v, 64, 1) + pltpu.roll(v, 7, 0)
+                v = pltpu.roll(v, 1, 0)
+                d1[9 * a + 3 * b : 9 * a + 3 * b + 3, :] = v[0:3]
+
+    def layers():
+        snrcv[1, j] = snsend[j]
+        @pl.when(has_l)
+        def _():
+            @pl.loop(0, GY)
+            def _(y):
+                sn_recv(-1, y).wait_recv()
+
+        @pl.when(has_r)
+        def _():
+            @pl.loop(0, GY)
+            def _(y):
+                sn_recv(1, y).wait_recv()
+
+        @pl.loop(1, GY)
+        def _(k):
+            sn_recv(0, lax.rem(j + k, GY)).wait_recv()
+
+        for d in range(3):
+            for y in range(8):
+                t = snrcv[d, y]
+                S6[2 * d, 2 * y : 2 * y + 2, :] = t[0:2]
+                S6[2 * d + 1, 2 * y : 2 * y + 2, :] = t[2:4]
+        for p in range(4):
+            CC[p, :, 0:128] = S6[p] + pltpu.roll(S6[p + 1], 64, 1)
+            CC[p, :, 128:256] = S6[p + 2]
+
+        for p in range(4):
+            keep = {0: jnp.where(has_l, 1.0, 0.0), 3: jnp.where(has_r, 1.0, 0.0)}.get(p)
+
+            for q in range(4):
+                rows = slice(q * 128, q * 128 + 128)
+                par = q // 2
+                jj = 2 * ((q % 2) * 8 + iota((8, 16, 256), 0)) + par
+                t = (iota((8, 16, 256), 2) & 63) - 2 * jj + 1
+                mask = (t >= 0) & (t < 4)
+                v = jnp.broadcast_to(CC[p][None], (8, 16, 256))
+                v = jnp.where(mask, v, 0.0).reshape(128, 256).astype(BF16)
+                r = dot(v, V[par])
+                z = row_before(r[:, 0:128]) + r[:, 128:256] + row_after(r[:, 256:384])
+                sig = 1.0 / (1.0 + jnp.exp(-z))
+                h = z * sig
+                if keep is not None:
+                    h = h * keep
+                H3[p, rows, 0:128] = row_before(h).astype(BF16)
+                H3[p, rows, 128:256] = h.astype(BF16)
+                H3[p, rows, 256:384] = row_after(h).astype(BF16)
+                if p in (1, 2):
+                    dz = dh[p - 1, rows, :] * (sig * (1.0 + z * (1.0 - sig)))
+                    DZ3[p - 1, rows, 0:128] = row_after(dz).astype(BF16)
+                    DZ3[p - 1, rows, 128:256] = dz.astype(BF16)
+                    DZ3[p - 1, rows, 256:384] = row_before(dz).astype(BF16)
+
+        for a in range(3):
+            acc[a] = dot(GT[0], H3[a]) + dot(GT[1], H3[a + 1])
+            if a == 2:
+                first_gradient()
+            for q in range((0, 4, 9)[a], (4, 9, 14)[a]):
+                other = term(2 * q + 1) if q < 13 else d1[...]
+                v = jnp.where(lane < 64, term(2 * q), other)
+                rsend[2 * q] = v[0:32].astype(BF16)
+                rsend[2 * q + 1] = v[32:64].astype(BF16)
+            c0, n = (0, 8, 18)[a], (8, 10, 10)[a]
+
+            @pl.loop(0, n)
+            def _(k):
+                m = c0 + lax.rem(me + k, n)
+                pl.when(m != me)(lambda: r1_send(m).start())
+
     def filler_one():
         for side, ok in x_sides:
             pl.when(ok)(lambda side=side: g_copy(side, False).wait_recv())
         windows(0, grcv[0])
         windows(3, grcv[1])
         back(0)
+        back(1)
 
     def filler_two():
-        back(1)
+        pl.when(j > 0)(layers)
 
     sweeps(RAD - 1, RAD)
     exchange(0, filler_one)
@@ -394,7 +528,7 @@
     for side, ok in y_sides:
         pl.when(ok)(lambda side=side: fy_copy(side, False).wait_recv())
 
-    pool = jnp.where(iota((FZ, 128), 0) // 4 == iota((FZ, 128), 1), 1.0 / 64.0, 0.0)
+    pool = jnp.where(iota((FZ, 128), 0) // 4 == iota((FZ, 128), 1), 1.0 / 64.0, 0.0).astype(BF16)
     row8 = iota((8, FZ), 0)
     sums = []
     total = None
@@ -419,7 +553,11 @@
         if x % 4 == 3:
             t = total + pltpu.roll(total, 7, 0)
             sums.append(t + pltpu.roll(t, 6, 0))
-    mean = dot(jnp.concatenate(sums, axis=0), pool, precision=lax.Precision.HIGHEST)
+    rest, mean = jnp.concatenate(sums, axis=0), 0.0
+    for _ in range(3):
+        part = rest.astype(BF16)
+        rest = rest - part.astype(F32)
+        mean = mean + dot(part, pool)
     for r in range(4):
         snsend[0, r : r + 1, :] = mean[4 * r : 4 * r + 1, :]
     snsend[0, 4:8, :] = jnp.zeros((4, 128), F32)
@@ -428,140 +566,12 @@
     stores = [
         pltpu.make_async_copy(a, b, out_s.at[k])
         for k, (a, b) in enumerate(
-            ((newl, newl_h), (prs, prs_h), (dw1o, dw1_h), (dw2o, dw2_h))
+            ((newl, newl_h), (prs, prs_h), (r3, sum_h))
         )
     ]
     stores[0].start()
     stores[1].start()
-    snrcv[1, j] = snsend[j]
-
-    @pl.when(has_l)
-    def _():
-        @pl.loop(0, GY)
-        def _(y):
-            sn_recv(-1, y).wait_recv()
-
-    @pl.when(has_r)
-    def _():
-        @pl.loop(0, GY)
-        def _(y):
-            sn_recv(1, y).wait_recv()
-
-    @pl.loop(1, GY)
-    def _(k):
-        sn_recv(0, lax.rem(j + k, GY)).wait_recv()
-
-    for d in range(3):
-        for y in range(8):
-            t = snrcv[d, y]
-            S6[2 * d, 2 * y : 2 * y + 2, :] = t[0:2]
-            S6[2 * d + 1, 2 * y : 2 * y + 2, :] = t[2:4]
-    for p in range(4):
-        CC[p, :, 0:128] = S6[p] + pltpu.roll(S6[p + 1], 64, 1)
-        CC[p, :, 128:256] = S6[p + 2]
-
-    for p in range(4):
-        keep = {0: jnp.where(has_l, 1.0, 0.0), 3: jnp.where(has_r, 1.0, 0.0)}.get(p)
-
-        for q in range(4):
-            rows = slice(q * 128, q * 128 + 128)
-            par = q // 2
-            jj = 2 * ((q % 2) * 8 + iota((8, 16, 256), 0)) + par
-            t = (iota((8, 16, 256), 2) & 63) - 2 * jj + 1
-            mask = (t >= 0) & (t < 4)
-            v = jnp.broadcast_to(CC[p][None], (8, 16, 256))
-            v = jnp.where(mask, v, 0.0).reshape(128, 256).astype(BF16)
-            r = dot(v, V[par])
-            z = row_before(r[:, 0:128]) + r[:, 128:256] + row_after(r[:, 256:384])
-            sig = 1.0 / (1.0 + jnp.exp(-z))
-            h = z * sig
-            if keep is not None:
-                h = h * keep
-            H3[p, rows, 0:128] = row_before(h).astype(BF16)
-            H3[p, rows, 128:256] = h.astype(BF16)
-            H3[p, rows, 256:384] = row_after(h).astype(BF16)
-            if p in (1, 2):
-                dz = dh[p - 1, rows, :] * (sig * (1.0 + z * (1.0 - sig)))
-                DZ3[p - 1, rows, 0:128] = row_after(dz).astype(BF16)
-                DZ3[p - 1, rows, 128:256] = dz.astype(BF16)
-                DZ3[p - 1, rows, 256:384] = row_before(dz).astype(BF16)
-
-    for a in range(3):
-        acc[a] = dot(GT[0], H3[a]) + dot(GT[1], H3[a + 1])
-
-    spread = jnp.where((iota((16, ROWS), 1) & 15) == iota((16, ROWS), 0), 1.0, 0.0).astype(BF16)
-    r_k = iota((256, ROWS), 0) & 63
-    r_c = iota((256, ROWS), 1)
-    jj = 2 * ((r_c & 255) // 16) + r_c // 256
-    t = r_k - 2 * jj + 1
-    near = (t >= 0) & (t < 4)
-    for x in range(2):
-        LT[x] = jnp.where(near, dot(CC[x + 1].T.astype(BF16), spread), 0.0).astype(BF16)
-    parts = []
-    for par in range(2):
-        cols = slice(par * 256, par * 256 + 256)
-        q = dot(LT[0, :, cols], DZ3[0, cols, :]) + dot(LT[1, :, cols], DZ3[1, cols, :])
-        q = q.reshape(4, 8, 8, 384)
-        parts.append([q[a].sum(0) for a in range(3)])
-    d1[...] = jnp.zeros((64, 128), F32)
-    for a in range(3):
-        u, w = parts[0][a], parts[1][a]
-        u = u + pltpu.roll(u, 4, 0)
-        w = w + pltpu.roll(w, 4, 0)
-        u = u + pltpu.roll(w, 2, 0)
-        for b in range(3):
-            v = u[:, b * 128 : (b + 1) * 128]
-            v = pltpu.roll(v, 64, 1) + pltpu.roll(v, 7, 0)
-            v = pltpu.roll(v, 1, 0)
-            d1[9 * a + 3 * b : 9 * a + 3 * b + 3, :] = v[0:3]
-
-    lane = iota((64, 128), 1)
-
-    def term(o):
-        a, b, c = o // 9, (o // 3) % 3, o % 3
-        r = (2 - c) * 64
-        cols = slice(b * 128, b * 128 + 128)
-        v = jnp.where(lane < 64, acc[a, r : r + 64, cols], acc[a, r + 64 : r + 128, cols])
-        return v + pltpu.roll(v, 64, 1)
-
-    for q in range(14):
-        other = term(2 * q + 1) if q < 13 else d1[...]
-        v = jnp.where(lane < 64, term(2 * q), other)
-        rsend[2 * q] = v[0:32].astype(BF16)
-        rsend[2 * q + 1] = v[32:64].astype(BF16)
-
-    def r1_send(m):
-        return pltpu.make_async_remote_copy(
-            src_ref=rsend.at[m], dst_ref=r1.at[me],
-            send_sem=r1_ss.at[m], recv_sem=r1_rs.at[me],
-            device_id=member(m), device_id_type=MESH,
-        )
-
-    def r1_recv(m):
-        return pltpu.make_async_remote_copy(
-            src_ref=rsend.at[0], dst_ref=r1.at[m],
-            send_sem=r1_ss.at[0], recv_sem=r1_rs.at[m],
-            device_id=member(m), device_id_type=MESH,
-        )
-
-    def r2_copy(k, slot):
-        return pltpu.make_async_remote_copy(
-            src_ref=r2.at[mez], dst_ref=r2.at[slot],
-            send_sem=r2_ss.at[k], recv_sem=r2_rs.at[slot],
-            device_id=zpeer(k), device_id_type=MESH,
-        )
-
-    def r3_copy(m, slot):
-        return pltpu.make_async_remote_copy(
-            src_ref=f3, dst_ref=r3.at[slot],
-            send_sem=r3_ss.at[m], recv_sem=r3_rs.at[slot],
-            device_id=member(m), device_id_type=MESH,
-        )
-
-    @pl.loop(1, GROUP)
-    def _(k):
-        m = lax.rem(me + k, GROUP)
-        pl.when(m < CHUNKS)(lambda: r1_send(m).start())
+    pl.when(j == 0)(layers)
 
     @pl.when(me < CHUNKS)
     def _():
@@ -597,16 +607,7 @@
         m = lax.rem(me + k, GROUP)
         pl.when(m < CHUNKS)(lambda: r3_copy(m, m).wait_recv())
 
-    for q in range(14):
-        v = jnp.concatenate([r3[2 * q], r3[2 * q + 1]], axis=0).astype(F32)
-        if q < 13:
-            dw2o[:, 128 * q : 128 * q + 128] = v
-        else:
-            dw2o[:, 128 * q : 128 * q + 64] = v[:, 0:64]
-            dw1o[...] = pltpu.roll(v, 64, 1)[0:27, 0:64]
-
     stores[2].start()
-    stores[3].start()
 
     for d in range(8):
         @pl.when(has(d))
@@ -638,6 +639,40 @@
             r2_copy(lax.rem(mez + k, ZS), mez).wait_send()
 
     for c in stores:
+        c.wait()
+
+
+def leave(
+    newl_h, prs_h, sum_h, newl_o, prs_o, dw1_o, dw2_o,
+    newl, prs, total, dw1, dw2, in_s, out_s,
+):
+    ins = [
+        pltpu.make_async_copy(a, b, in_s.at[k])
+        for k, (a, b) in enumerate(((sum_h, total), (newl_h, newl), (prs_h, prs)))
+    ]
+    outs = [
+        pltpu.make_async_copy(a, b, out_s.at[k])
+        for k, (a, b) in enumerate(
+            ((newl, newl_o), (prs, prs_o), (dw1, dw1_o), (dw2, dw2_o))
+        )
+    ]
+    for c in ins:
+        c.start()
+    ins[0].wait()
+    for q in range(14):
+        v = jnp.concatenate([total[2 * q], total[2 * q + 1]], axis=0).astype(F32)
+        if q < 13:
+            dw2[:, 128 * q : 128 * q + 128] = v
+        else:
+            dw2[:, 128 * q : 128 * q + 64] = v[:, 0:64]
+            dw1[...] = pltpu.roll(v, 64, 1)[0:27, 0:64]
+    outs[3].start()
+    outs[2].start()
+    ins[1].wait()
+    outs[0].start()
+    ins[2].wait()
+    outs[1].start()
+    for c in outs:
         c.wait()
 
 
@@ -656,17 +691,16 @@
         jax.ShapeDtypeStruct((27, 64), F32),
         jax.ShapeDtypeStruct((64, 1728), F32),
     )
+    sums = jax.ShapeDtypeStruct((CHUNKS, 32, 128), BF16)
     results = pl.pallas_call(
         kernel,
-        out_shape=shapes,
+        out_shape=shapes[:2] + (sums,),
         in_specs=[hbm, hbm, hbm, vm, sm, vm, hbm, hbm],
-        out_specs=(hbm,) * 4,
+        out_specs=(hbm,) * 3,
         scratch_shapes=[
             pltpu.VMEM((8, 8, FZ), F32),
             pltpu.VMEM((8, 8, FZ), F32),
-            pltpu.VMEM((27, 64), F32),
-            pltpu.VMEM((64, 1728), F32),
-            dma((4,)),
+            dma((3,)),
             pltpu.VMEM((8, 8, FZ), F32),
             pltpu.VMEM((8, 8, FZ), F32),
             pltpu.VMEM((8, 8, FZ), F32),
@@ -713,6 +747,22 @@
             collective_id=0, has_side_effects=True, vmem_limit_bytes=60 * 1024 * 1024
         ),
     )(source, stiffness, level_set, snap, buffer_order, first_weight, second_weight.T, g)
+    results = pl.pallas_call(
+        leave,
+        out_shape=shapes,
+        in_specs=[hbm] * 3,
+        out_specs=(hbm,) * 4,
+        scratch_shapes=[
+            pltpu.VMEM(shapes[0].shape, F32),
+            pltpu.VMEM(shapes[1].shape, F32),
+            pltpu.VMEM(sums.shape, BF16),
+            pltpu.VMEM(shapes[2].shape, F32),
+            pltpu.VMEM(shapes[3].shape, F32),
+            dma((3,)),
+            dma((4,)),
+        ],
+        compiler_params=pltpu.CompilerParams(vmem_limit_bytes=60 * 1024 * 1024),
+    )(*results)
     return results[0], results[1], results[2], results[3].T
 
 

time: 71.6 us -> 68.8 us (0.961)
  local copies, waits for them, and re-layouts: 4.64 us -> 0 us
  Pallas kernels: 66.1 us -> 67.8 us
    unnamed x8 -> x0, local copies, waits for them, and re-layouts: 4.64 us -> none
    pallas_call x1 -> x2, Pallas kernels: 66.1 us -> 67.8 us  [the longest x1 66 us: per_device(): pl.pallas_call(kernel, out_shape=shapes[:2] + (sums,), in_specs=[hbm, hbm...]
where the time goes in v3:
time: 68.8 us; the launch traced here: 68.7 us
  Pallas kernels  67.8 us (99%)
  between operations  0.82 us (1%)
    pallas_call x1, Pallas kernels, per_device(): pl.pallas_call(kernel, out_shape=shapes[:2] + (sums,), in_specs=[hbm, hbm...  66 us
    pallas_call x1, Pallas kernels, per_device(): pl.pallas_call(leave, out_shape=shapes, in_specs=[hbm] * 3, out_specs=(hb...  1.84 us

profile of v3, /device:TPU:1, one launch (start us, length us, event | category | flops | bytes accessed | tf_op | source)
XLA Modules:
  0.0 68.7 jit_solution(10068749380646769891)
XLA Ops:
  0.6 66.0 %shard_map.111 = (f32[8,8,256]{2,1,0:T(8,128)}, f32[8,8,256]{2,1,0:T(8,128)}, bf16[28,32,128]{2,1,0:T(8,128)(2,1)}) custom-call(f32[8,8,256]{2,1,0:T(8,128)} %src_h.1, f32[8,8,256]{2,1,0:T(8,128)} %stf_h.1, f32[8,8,256]{2,1,0:T(8,128)} %lev_h.1, bf16[8,4,64]{2,1,0:T(4,128)(2,1)} %bitcast.6, s32[8]{0:T(128)} %order.1, bf16[27,64]{1,0:T(8,128)(2,1)} %w1.1, ...), custom_call_target="tpu_custom_call" | custom-call | tf_op jit(solution)/shard_map/pallas_call | solution.py:695
  66.6 1.8 %shard_map.112 = (f32[8,8,256]{2,1,0:T(8,128)}, f32[8,8,256]{2,1,0:T(8,128)}, f32[27,64]{1,0:T(8,128)}, f32[64,1728]{1,0:T(8,128)}) custom-call(f32[8,8,256]{2,1,0:T(8,128)} %get-tuple-element.11.newl_h, f32[8,8,256]{2,1,0:T(8,128)} %get-tuple-element.12.prs_h, bf16[28,32,128]{2,1,0:T(8,128)(2,1)} %get-tuple-element.13.sum_h), custom_call_target="tpu_custom_call" | custom-call | tf_op jit(solution)/shard_map/pallas_call | solution.py:750

commit v4 on v3

--- a/solution.py
+++ b/solution.py
@@ -84,6 +84,7 @@
     czl, cx = j // 4, j % 4
     me = cy * 8 + cc * 4 + cx
     mez = czh * 2 + czl
+    mine = lax.rem(3 * me, GROUP)
 
     def member(m):
         return ((m // 8) * 8 + czh * 2 + (m // 4) % 2, czl * 4 + m % 4)
@@ -105,6 +106,14 @@
     def greet(dev):
         pl.semaphore_signal(bar, inc=1, device_id=dev, device_id_type=MESH)
 
+    @pl.loop(1, ZS)
+    def _(k):
+        greet(zpeer(lax.rem(mez + k, ZS)))
+
+    @pl.loop(1, GROUP)
+    def _(k):
+        greet(member(lax.rem(me + k, GROUP)))
+
     @pl.when(has_l)
     def _():
         @pl.loop(0, GY)
@@ -121,13 +130,6 @@
     def _(k):
         greet((i, lax.rem(j + k, GY)))
 
-    @pl.loop(1, GROUP)
-    def _(k):
-        greet(member(lax.rem(me + k, GROUP)))
-
-    @pl.loop(1, ZS)
-    def _(k):
-        greet(zpeer(lax.rem(mez + k, ZS)))
 
     for c in loads[:4]:
         c.wait()
@@ -247,9 +249,6 @@
         pl.when(ok)(lambda side=side: fx_copy(side, True).start())
     for side, ok in y_sides:
         pl.when(ok)(lambda side=side: fy_copy(side, True).start())
-    for side, ok in x_sides:
-        pl.when(ok)(lambda side=side: g_copy(side, True).start())
-
     def each_snap(lo, hi, act):
         @pl.loop(lo, hi)
         def _(s):
@@ -257,7 +256,6 @@
             pl.when(s != j)(lambda: act(0, s))
             pl.when(has_r)(lambda: act(1, s))
 
-    each_snap(1, GY, lambda d, s: sn_send(d, s).start())
 
     loads[4].wait()
     w2p[:, 0:1728] = w2[...].astype(F32)
@@ -317,10 +315,6 @@
                 r = (((t - 1) % 2) * 16 + (t - 1) // 2) * 16
                 W[plane, r : r + 16, 128:256] = tile
 
-    for x in range(2):
-        windows(x + 1, g[x])
-        GT[x] = W[x + 1].T
-
     for d, (dx, dy) in enumerate(DIRS):
         lo, n = tile_rows(dx, RAD if dy == 0 else RAD - 1)
         xs, ys = pl.ds(8 + 8 * dx + lo, n), pl.ds(8 + 8 * dy, 8)
@@ -386,7 +380,7 @@
         return pltpu.make_async_remote_copy(
             src_ref=rsend.at[m], dst_ref=r1.at[me],
             send_sem=r1_ss.at[m], recv_sem=r1_rs.at[me],
-            device_id=member(m), device_id_type=MESH,
+            device_id=member(lax.rem(11 * m, GROUP)), device_id_type=MESH,
         )
 
     def r1_recv(m):
@@ -504,18 +498,23 @@
             @pl.loop(0, n)
             def _(k):
                 m = c0 + lax.rem(me + k, n)
-                pl.when(m != me)(lambda: r1_send(m).start())
+                pl.when(m != mine)(lambda: r1_send(m).start())
 
     def filler_one():
+        each_snap(1, GY, lambda d, s: sn_send(d, s).start())
+        for side, ok in x_sides:
+            pl.when(ok)(lambda side=side: g_copy(side, True).start())
+        for x in range(2):
+            windows(x + 1, g[x])
+            GT[x] = W[x + 1].T
+
+    def filler_two():
         for side, ok in x_sides:
             pl.when(ok)(lambda side=side: g_copy(side, False).wait_recv())
         windows(0, grcv[0])
         windows(3, grcv[1])
         back(0)
         back(1)
-
-    def filler_two():
-        pl.when(j > 0)(layers)
 
     sweeps(RAD - 1, RAD)
     exchange(0, filler_one)
@@ -571,43 +570,7 @@
     ]
     stores[0].start()
     stores[1].start()
-    pl.when(j == 0)(layers)
-
-    @pl.when(me < CHUNKS)
-    def _():
-        def add(k, total):
-            m = lax.rem(me + k, GROUP)
-            r1_recv(m).wait_recv()
-            return total + r1[m].astype(F32)
-
-        r2[mez] = lax.fori_loop(1, GROUP, add, rsend[me].astype(F32))
-
-        @pl.loop(1, ZS)
-        def _(k):
-            r2_copy(lax.rem(mez + k, ZS), mez).start()
-
-        @pl.loop(1, ZS)
-        def _(k):
-            m = lax.rem(mez + k, ZS)
-            r2_copy(m, m).wait_recv()
-
-        total = r2[0]
-        for k in range(1, ZS):
-            total = total + r2[k]
-        f3[...] = total.astype(BF16)
-
-        @pl.loop(1, GROUP)
-        def _(k):
-            r3_copy(lax.rem(me + k, GROUP), me).start()
-
-        r3[me] = f3[...]
-
-    @pl.loop(1, GROUP)
-    def _(k):
-        m = lax.rem(me + k, GROUP)
-        pl.when(m < CHUNKS)(lambda: r3_copy(m, m).wait_recv())
-
-    stores[2].start()
+    layers()
 
     for d in range(8):
         @pl.when(has(d))
@@ -626,17 +589,56 @@
         pl.when(ok)(lambda side=side: fy_copy(side, True).wait_send())
     each_snap(0, GY, lambda d, s: sn_send(d, s).wait_send())
 
-    @pl.loop(1, GROUP)
-    def _(k):
-        m = lax.rem(me + k, GROUP)
-        pl.when(m < CHUNKS)(lambda: r1_send(m).wait_send())
-        pl.when(me < CHUNKS)(lambda: r3_copy(m, me).wait_send())
-
-    @pl.when(me < CHUNKS)
+    @pl.when(mine < CHUNKS)
+    def _():
+        def add(k, total):
+            m = lax.rem(me + k, GROUP)
+            r1_recv(m).wait_recv()
+            return total + r1[m].astype(F32)
+
+        r2[mez] = lax.fori_loop(1, GROUP, add, rsend[mine].astype(F32))
+
+        @pl.loop(1, ZS)
+        def _(k):
+            r2_copy(lax.rem(mez + k, ZS), mez).start()
+
+        @pl.loop(1, ZS)
+        def _(k):
+            m = lax.rem(mez + k, ZS)
+            r2_copy(m, m).wait_recv()
+
+        total = r2[0]
+        for k in range(1, ZS):
+            total = total + r2[k]
+        f3[...] = total.astype(BF16)
+
+        @pl.loop(1, GROUP)
+        def _(k):
+            r3_copy(lax.rem(me + k, GROUP), mine).start()
+
+        r3[mine] = f3[...]
+
+    @pl.loop(0, CHUNKS)
+    def _(m):
+        pl.when(m != mine)(lambda: r1_send(m).wait_send())
+
+    @pl.when(mine < CHUNKS)
     def _():
         @pl.loop(1, ZS)
         def _(k):
             r2_copy(lax.rem(mez + k, ZS), mez).wait_send()
+
+    @pl.loop(0, CHUNKS)
+    def _(m):
+        pl.when(m != mine)(lambda: r3_copy(m, m).wait_recv())
+
+    stores[2].start()
+
+    @pl.when(mine < CHUNKS)
+    def _():
+        @pl.loop(1, GROUP)
+        def _(k):
+            r3_copy(lax.rem(me + k, GROUP), mine).wait_send()
 
     for c in stores:
         c.wait()

time: 68.8 us -> 66.6 us (0.968)
  Pallas kernels: 67.8 us -> 65.8 us
    pallas_call x1, Pallas kernels: 66 us -> 64 us  [per_device(): pl.pallas_call(kernel, out_shape=shapes[:2] + (sums,), in_specs=[hbm, hbm...]
where the time goes in v4:
time: 66.6 us; the launch traced here: 66.4 us
  Pallas kernels  65.8 us (99%)
    pallas_call x1, Pallas kernels, per_device(): pl.pallas_call(kernel, out_shape=shapes[:2] + (sums,), in_specs=[hbm, hbm...  64 us
    pallas_call x1, Pallas kernels, per_device(): pl.pallas_call(leave, out_shape=shapes, in_specs=[hbm] * 3, out_specs=(hb...  1.84 us

profile of v4, /device:TPU:1, one launch (start us, length us, event | category | flops | bytes accessed | tf_op | source)
XLA Modules:
  0.0 66.4 jit_solution(8748207814072067747)
XLA Ops:
  0.6 64.0 %shard_map.111 = (f32[8,8,256]{2,1,0:T(8,128)}, f32[8,8,256]{2,1,0:T(8,128)}, bf16[28,32,128]{2,1,0:T(8,128)(2,1)}) custom-call(f32[8,8,256]{2,1,0:T(8,128)} %src_h.1, f32[8,8,256]{2,1,0:T(8,128)} %stf_h.1, f32[8,8,256]{2,1,0:T(8,128)} %lev_h.1, bf16[8,4,64]{2,1,0:T(4,128)(2,1)} %bitcast.6, s32[8]{0:T(128)} %order.1, bf16[27,64]{1,0:T(8,128)(2,1)} %w1.1, ...), custom_call_target="tpu_custom_call" | custom-call | tf_op jit(solution)/shard_map/pallas_call | solution.py:697
  64.6 1.8 %shard_map.112 = (f32[8,8,256]{2,1,0:T(8,128)}, f32[8,8,256]{2,1,0:T(8,128)}, f32[27,64]{1,0:T(8,128)}, f32[64,1728]{1,0:T(8,128)}) custom-call(f32[8,8,256]{2,1,0:T(8,128)} %get-tuple-element.11.newl_h, f32[8,8,256]{2,1,0:T(8,128)} %get-tuple-element.12.prs_h, bf16[28,32,128]{2,1,0:T(8,128)(2,1)} %get-tuple-element.13.sum_h), custom_call_target="tpu_custom_call" | custom-call | tf_op jit(solution)/shard_map/pallas_call | solution.py:752

commit v5 on v4

--- a/solution.py
+++ b/solution.py
@@ -20,6 +20,9 @@
 ZS = 8
 DIRS = [(dx, dy) for dx in (-1, 0, 1) for dy in (-1, 0, 1) if (dx, dy) != (0, 0)]
 
+FAR_FIRST = (0, 2, 5, 7, 1, 6, 3, 4)
+NEAR_FIRST = FAR_FIRST[::-1]
+
 
 def dot(a, b, dims=((1,), (0,)), precision=None):
     return lax.dot_general(
@@ -56,10 +59,10 @@
 
 
 def kernel(
-    src_h, stf_h, lev_h, snp, order, w1, w2_h, g_h,
+    src_h, stf_h, lev_h, snp_h, order, w1_h, w2_h, g_h,
     newl_h, prs_h, sum_h,
     newl, prs, out_s,
-    src, stf, lev, w2, g, w2p, in_s,
+    src, stf, lev, w2, g, snp, w1, w2p, in_s,
     A, B, PP, absend, abrcv, psend, prcv, fysend, fxr, fyr,
     snsend, snrcv, grcv, W, GT, BT, V, w1s, S6, CC, H3, DZ3, LT, dh, acc, d1,
     rsend, r1, r2, f3, r3,
@@ -95,7 +98,10 @@
     loads = [
         pltpu.make_async_copy(a, b, in_s.at[k])
         for k, (a, b) in enumerate(
-            ((src_h, src), (stf_h, stf), (lev_h, lev), (g_h, g), (w2_h, w2))
+            (
+                (src_h, src), (stf_h, stf), (lev_h, lev), (g_h, g), (w2_h, w2),
+                (snp_h, snp), (w1_h, w1),
+            )
         )
     ]
     for c in loads:
@@ -129,7 +135,6 @@
     @pl.loop(1, GY)
     def _(k):
         greet((i, lax.rem(j + k, GY)))
-
 
     for c in loads[:4]:
         c.wait()
@@ -171,6 +176,7 @@
     def _():
         fyr[1] = jnp.zeros((T, FZ), F32)
 
+    loads[5].wait()
     snsend[...] = jnp.zeros((8, 8, 128), F32)
     for s in range(1, 8):
         snsend[s, 0:4, 0:64] = snp[order[s]].astype(F32)
@@ -243,7 +249,7 @@
     x_sides = ((0, has_l), (1, has_r))
     y_sides = ((0, has_y[-1]), (1, has_y[1]))
 
-    for d in range(8):
+    for d in FAR_FIRST:
         pl.when(has(d))(lambda d=d: ab_copy(d, True).start())
     for side, ok in x_sides:
         pl.when(ok)(lambda side=side: fx_copy(side, True).start())
@@ -279,6 +285,7 @@
             for k, v in enumerate(tiles):
                 BT[a, 64 * k : 64 * k + 64, 128 * b : 128 * b + 128] = v.astype(BF16)
 
+    loads[6].wait()
     w1s[...] = jnp.zeros((32, 128), F32)
     w1s[0:27, 0:64] = w1[...].astype(F32)
     w1d = w1s[...]
@@ -315,7 +322,8 @@
                 r = (((t - 1) % 2) * 16 + (t - 1) // 2) * 16
                 W[plane, r : r + 16, 128:256] = tile
 
-    for d, (dx, dy) in enumerate(DIRS):
+    for d in NEAR_FIRST:
+        dx, dy = DIRS[d]
         lo, n = tile_rows(dx, RAD if dy == 0 else RAD - 1)
         xs, ys = pl.ds(8 + 8 * dx + lo, n), pl.ds(8 + 8 * dy, 8)
 
@@ -343,10 +351,11 @@
     def exchange(e, filler):
         own = PP[8:16, 8:16, :]
         psend[e] = own.reshape(4, 16, FZ).astype(BF16)
-        for d in range(8):
+        for d in FAR_FIRST:
             pl.when(has(d))(lambda d=d: p_copy(e, d, True).start())
         filler()
-        for d, (dx, dy) in enumerate(DIRS):
+        for d in NEAR_FIRST:
+            dx, dy = DIRS[d]
             lo, n = tile_rows(dx, 8 if dy == 0 else 6)
             xs, ys = pl.ds(8 + 8 * dx + lo, n), pl.ds(8 + 8 * dy, 8)
 
@@ -683,7 +692,6 @@
 ):
     snap = snap_buffer.reshape(8, 4, 64)
     g = out_grad.reshape(2, 16, 4096)
-    vm = pl.BlockSpec(memory_space=pltpu.VMEM)
     sm = pl.BlockSpec(memory_space=pltpu.SMEM)
     hbm = pl.BlockSpec(memory_space=pltpu.HBM)
     dma = pltpu.SemaphoreType.DMA
@@ -697,7 +705,7 @@
     results = pl.pallas_call(
         kernel,
         out_shape=shapes[:2] + (sums,),
-        in_specs=[hbm, hbm, hbm, vm, sm, vm, hbm, hbm],
+        in_specs=[hbm, hbm, hbm, hbm, sm, hbm, hbm, hbm],
         out_specs=(hbm,) * 3,
         scratch_shapes=[
             pltpu.VMEM((8, 8, FZ), F32),
@@ -708,8 +716,10 @@
             pltpu.VMEM((8, 8, FZ), F32),
             pltpu.VMEM((64, 1728), BF16),
             pltpu.VMEM((2, 16, 4096), BF16),
+            pltpu.VMEM((8, 4, 64), BF16),
+            pltpu.VMEM((27, 64), BF16),
             pltpu.VMEM((64, 1792), F32),
-            dma((5,)),
+            dma((7,)),
             pltpu.VMEM((24, 24, FZ), F32),
             pltpu.VMEM((24, 24, FZ), F32),
             pltpu.VMEM((24, 24, FZ), F32),

time: 66.6 us -> 65 us (0.976)
  Pallas kernels: 65.8 us -> 64.3 us
    pallas_call x1, Pallas kernels: 64 us -> 62.4 us  [per_device(): pl.pallas_call(kernel, out_shape=shapes[:2] + (sums,), in_specs=[hbm, hbm...]
where the time goes in v5:
time: 65 us; the launch traced here: 64.9 us
  Pallas kernels  64.3 us (99%)
    pallas_call x1, Pallas kernels, per_device(): pl.pallas_call(kernel, out_shape=shapes[:2] + (sums,), in_specs=[hbm, hbm...  62.4 us
    pallas_call x1, Pallas kernels, per_device(): pl.pallas_call(leave, out_shape=shapes, in_specs=[hbm] * 3, out_specs=(hb...  1.84 us

profile of v5, /device:TPU:1, one launch (start us, length us, event | category | flops | bytes accessed | tf_op | source)
XLA Modules:
  0.0 64.9 jit_solution(4922765096609243354)
XLA Ops:
  0.6 62.4 %shard_map.111 = (f32[8,8,256]{2,1,0:T(8,128)}, f32[8,8,256]{2,1,0:T(8,128)}, bf16[28,32,128]{2,1,0:T(8,128)(2,1)}) custom-call(f32[8,8,256]{2,1,0:T(8,128)} %src_h.1, f32[8,8,256]{2,1,0:T(8,128)} %stf_h.1, f32[8,8,256]{2,1,0:T(8,128)} %lev_h.1, bf16[8,4,64]{2,1,0:T(4,128)(2,1)} %bitcast.6, s32[8]{0:T(128)} %order.1, bf16[27,64]{1,0:T(8,128)(2,1)} %w1_h.1, ...), custom_call_target="tpu_custom_call" | custom-call | tf_op jit(solution)/shard_map/pallas_call | solution.py:705
  63.1 1.8 %shard_map.112 = (f32[8,8,256]{2,1,0:T(8,128)}, f32[8,8,256]{2,1,0:T(8,128)}, f32[27,64]{1,0:T(8,128)}, f32[64,1728]{1,0:T(8,128)}) custom-call(f32[8,8,256]{2,1,0:T(8,128)} %get-tuple-element.11.newl_h, f32[8,8,256]{2,1,0:T(8,128)} %get-tuple-element.12.prs_h, bf16[28,32,128]{2,1,0:T(8,128)(2,1)} %get-tuple-element.13.sum_h), custom_call_target="tpu_custom_call" | custom-call | tf_op jit(solution)/shard_map/pallas_call | solution.py:762

commit v6 on v5

--- a/solution.py
+++ b/solution.py
@@ -607,12 +607,9 @@
 
         r2[mez] = lax.fori_loop(1, GROUP, add, rsend[mine].astype(F32))
 
-        @pl.loop(1, ZS)
-        def _(k):
+        for k in (4, 3, 5, 2, 6, 1, 7):
             r2_copy(lax.rem(mez + k, ZS), mez).start()
-
-        @pl.loop(1, ZS)
-        def _(k):
+        for k in (7, 1, 6, 2, 5, 3, 4):
             m = lax.rem(mez + k, ZS)
             r2_copy(m, m).wait_recv()
 
@@ -621,9 +618,14 @@
             total = total + r2[k]
         f3[...] = total.astype(BF16)
 
-        @pl.loop(1, GROUP)
-        def _(k):
-            r3_copy(lax.rem(me + k, GROUP), mine).start()
+        for dy, dx in sorted(
+            ((y, x) for y in range(4) for x in range(4)),
+            key=lambda v: -min(v[0], 4 - v[0]) - min(v[1], 4 - v[1]),
+        ):
+            for dc in range(2):
+                if (dy, dx, dc) != (0, 0, 0):
+                    y, x, c = lax.rem(cy + dy, 4), lax.rem(cx + dx, 4), lax.rem(cc + dc, 2)
+                    r3_copy(y * 8 + c * 4 + x, mine).start()
 
         r3[mine] = f3[...]
 

time: 65 us -> 64.4 us (level)
  no operation moved by 1% of the time
where the time goes in v6:
time: 64.4 us; the launch traced here: 64.3 us
  Pallas kernels  63.7 us (99%)
    pallas_call x1, Pallas kernels, per_device(): pl.pallas_call(kernel, out_shape=shapes[:2] + (sums,), in_specs=[hbm, hbm...  61.8 us
    pallas_call x1, Pallas kernels, per_device(): pl.pallas_call(leave, out_shape=shapes, in_specs=[hbm] * 3, out_specs=(hb...  1.84 us

profile of v6, /device:TPU:1, one launch (start us, length us, event | category | flops | bytes accessed | tf_op | source)
XLA Modules:
  0.0 64.3 jit_solution(7923824840046019666)
XLA Ops:
  0.6 61.8 %shard_map.111 = (f32[8,8,256]{2,1,0:T(8,128)}, f32[8,8,256]{2,1,0:T(8,128)}, bf16[28,32,128]{2,1,0:T(8,128)(2,1)}) custom-call(f32[8,8,256]{2,1,0:T(8,128)} %src_h.1, f32[8,8,256]{2,1,0:T(8,128)} %stf_h.1, f32[8,8,256]{2,1,0:T(8,128)} %lev_h.1, bf16[8,4,64]{2,1,0:T(4,128)(2,1)} %bitcast.6, s32[8]{0:T(128)} %order.1, bf16[27,64]{1,0:T(8,128)(2,1)} %w1_h.1, ...), custom_call_target="tpu_custom_call" | custom-call | tf_op jit(solution)/shard_map/pallas_call | solution.py:707
  62.5 1.8 %shard_map.112 = (f32[8,8,256]{2,1,0:T(8,128)}, f32[8,8,256]{2,1,0:T(8,128)}, f32[27,64]{1,0:T(8,128)}, f32[64,1728]{1,0:T(8,128)}) custom-call(f32[8,8,256]{2,1,0:T(8,128)} %get-tuple-element.11.newl_h, f32[8,8,256]{2,1,0:T(8,128)} %get-tuple-element.12.prs_h, bf16[28,32,128]{2,1,0:T(8,128)(2,1)} %get-tuple-element.13.sum_h), custom_call_target="tpu_custom_call" | custom-call | tf_op jit(solution)/shard_map/pallas_call | solution.py:764
